TPU v7x, 32 devices: a whole 2x2x4 slice. The times are simulated.
32 devices in a mesh: lat: 8 (over z, y), lon: 4 (over x, core).
Axes of the slice: x: 2, y: 2, z: 4, core: 2. Of those that a mesh axis runs over, the one named last changes fastest.
Arguments:
- tokens: bfloat16 [24, 256, 512], P('lat', 'lon'), may hold values from -6 to 6
- ocean_count: int32 [24, 4], P('lat', 'lon'), may hold values from 1 to 64
- w_qkv: bfloat16 [512, 1536], replicated, may hold values from -0.25 to 0.25
- w_out: bfloat16 [512, 512], replicated, may hold values from -0.25 to 0.25
- w_up: bfloat16 [512, 1024], replicated, may hold values from -0.25 to 0.25
- w_down: bfloat16 [1024, 512], replicated, may hold values from -0.1875 to 0.1875
- cotangent: bfloat16 [24, 256, 512], P('lat', 'lon'), may hold values from -6 to 6
Outputs:
- block_out: bfloat16 [24, 256, 512], P('lat', 'lon')
- grad_tokens: bfloat16 [24, 256, 512], P('lat', 'lon')
- grad_qkv: float32 [512, 1536], P('lat')
- grad_out: float32 [512, 512], P('lat')
- grad_up: float32 [512, 1024], P('lat')
- grad_down: float32 [1024, 512], P('lat')
Inputs may be any that keep to these rules, and one draw needn't show every extreme that they name: The ocean patches of row r in sector s are that sector's first ocean_count[r, s] positions; the others are land.
All inputs are finite; a program needn't handle non-finite values.
Results may differ from a plain program's by a relative error of at most 0.023.
Values may be sent and summed in bfloat16 or wider, within the bound.
A program may use at most 64 MiB of HBM per device.

v0:
```python
import math

import jax
import jax.numpy as jnp
from jax import lax
from jax.sharding import PartitionSpec as P

HEAD_DIM = 64


SOFTMAX_SCALE = 8.0


def widen(values):
    return lax.optimization_barrier(values).astype(jnp.float32)


def elementwise_product(pattern, left_side, right_side):
    return jnp.einsum(pattern, left_side, right_side, preferred_element_type=jnp.float32)


def flatten(values):
    return values.reshape(-1, values.shape[-1])


def layer_norm(values):
    average = jnp.mean(values, axis=-1, keepdims=True)
    centered = values - average
    variance = jnp.mean(centered * centered, axis=-1, keepdims=True)
    return centered * lax.rsqrt(variance + 1e-05)


def split_heads(values, head_count):
    return values.reshape(values.shape[:-1] + (head_count, values.shape[-1] // head_count))


def head_norm(values, head_count):
    shaped = split_heads(values, head_count)
    scaled = shaped * lax.rsqrt(jnp.mean(shaped * shaped, axis=-1, keepdims=True) + 1e-06)
    return scaled.reshape(values.shape)


def project_in(tokens, w_qkv, head_count):
    model_width = tokens.shape[-1]
    normed = layer_norm(tokens.astype(jnp.float32)).astype(jnp.bfloat16)
    projected = elementwise_product("...d,de->...e", normed, w_qkv)
    query_raw = projected[..., :model_width]
    key_raw = projected[..., model_width : 2 * model_width]
    query_b = head_norm(query_raw, head_count).astype(jnp.bfloat16)
    key_value = jnp.concatenate(
        [head_norm(key_raw, head_count), projected[..., 2 * model_width :]], axis=-1
    ).astype(jnp.bfloat16)
    return (normed, query_b, key_value, query_raw, key_raw)


def row_scores(query_b, key_value, key_land_mask, head_count):
    model_width = query_b.shape[-1]
    head_features = model_width // head_count
    query_per_head = split_heads(query_b, head_count)
    key_per_head = split_heads(key_value[:, :model_width], head_count)
    unmasked_logits = elementwise_product("mvp,lvp->vml", query_per_head, key_per_head) * (
        SOFTMAX_SCALE / head_features
    )
    return (
        jnp.exp(unmasked_logits - SOFTMAX_SCALE) * key_land_mask.astype(jnp.float32)[None, None, :]
    )


def attend_row(query_b, key_value, key_land_mask, head_count):
    model_width = query_b.shape[-1]
    expscore = row_scores(query_b, key_value, key_land_mask, head_count)
    value_heads = split_heads(key_value[:, model_width:], head_count)
    numerator = elementwise_product("hqk,khc->qhc", expscore.astype(jnp.bfloat16), value_heads)
    row_total = jnp.transpose(jnp.sum(expscore, axis=-1))
    return (numerator.reshape(numerator.shape[0], model_width), row_total)


def attend_row_back(
    query_b, key_value, key_land_mask, row_total, grad_b, gradient_correction, head_count
):
    model_width = query_b.shape[-1]
    head_features = model_width // head_count
    expscore = row_scores(query_b, key_value, key_land_mask, head_count)
    row_attention_weight = expscore / jnp.transpose(row_total)[:, :, None]
    query_per_head = split_heads(query_b, head_count)
    key_per_head = split_heads(key_value[:, :model_width], head_count)
    value_heads = split_heads(key_value[:, model_width:], head_count)
    grad_heads = split_heads(grad_b, head_count)
    gradient_weights = elementwise_product("mvp,lvp->vml", grad_heads, value_heads)
    gradient_logits = (
        row_attention_weight
        * (gradient_weights - jnp.transpose(gradient_correction)[:, :, None])
        * (SOFTMAX_SCALE / head_features)
    ).astype(jnp.bfloat16)
    grad_query = elementwise_product("hqk,khc->qhc", gradient_logits, key_per_head).reshape(
        -1, model_width
    )
    grad_key = elementwise_product("hqk,qhc->khc", gradient_logits, query_per_head).reshape(
        -1, model_width
    )
    grad_value = elementwise_product(
        "hqk,qhc->khc", row_attention_weight.astype(jnp.bfloat16), grad_heads
    ).reshape(-1, model_width)
    return (grad_query, jnp.concatenate([grad_key, grad_value], axis=-1))


def forward_tail(tokens, attended_b, ocean_mask, w_out, w_up, w_down):
    middle = tokens.astype(jnp.float32) + ocean_mask[..., None] * elementwise_product(
        "...d,de->...e", attended_b, w_out
    )
    normed_two = layer_norm(middle).astype(jnp.bfloat16)
    lifted = elementwise_product("...d,df->...f", normed_two, w_up)
    active = jax.nn.gelu(lifted).astype(jnp.bfloat16)
    block_out = (
        middle + ocean_mask[..., None] * elementwise_product("...f,fd->...d", active, w_down)
    ).astype(jnp.bfloat16)
    return (block_out, (middle, normed_two, lifted, active))


def backward_tail(cotangent, ocean_mask, attended_b, tail_saved, w_out, w_up, w_down):
    middle, normed_two, lifted, active = tail_saved
    upstream = cotangent.astype(jnp.float32)
    grad_branch = (ocean_mask[..., None] * upstream).astype(jnp.bfloat16)
    grad_active = elementwise_product("...d,fd->...f", grad_branch, w_down)
    grad_lifted = jax.vjp(jax.nn.gelu, lifted)[1](grad_active)[0].astype(jnp.bfloat16)
    grad_normed = elementwise_product("...f,df->...d", grad_lifted, w_up)
    grad_middle = upstream + jax.vjp(layer_norm, middle)[1](grad_normed)[0]
    grad_attn = (ocean_mask[..., None] * grad_middle).astype(jnp.bfloat16)
    grad_attended = elementwise_product("...e,de->...d", grad_attn, w_out).astype(jnp.bfloat16)
    term_out = elementwise_product("td,te->de", flatten(attended_b), flatten(grad_attn))
    term_up = elementwise_product("td,tf->df", flatten(normed_two), flatten(grad_lifted))
    term_down = elementwise_product("tf,td->fd", flatten(active), flatten(grad_branch))
    return (grad_middle, grad_attended, (term_out, term_up, term_down))


def backward_head(
    tokens, normed, query_raw, key_raw, grad_query, grad_kv, grad_middle, w_qkv, head_count
):
    model_width = tokens.shape[-1]
    grad_qraw = jax.vjp(lambda values: head_norm(values, head_count), query_raw)[1](grad_query)[0]
    grad_kraw = jax.vjp(lambda values: head_norm(values, head_count), key_raw)[1](
        grad_kv[..., :model_width]
    )[0]
    grad_projected = jnp.concatenate(
        [grad_qraw, grad_kraw, grad_kv[..., model_width:]], axis=-1
    ).astype(jnp.bfloat16)
    term_qkv = elementwise_product("td,te->de", flatten(normed), flatten(grad_projected))
    grad_normed = elementwise_product("...e,de->...d", grad_projected, w_qkv)
    grad_layer = jax.vjp(layer_norm, tokens.astype(jnp.float32))[1](grad_normed)[0]
    return ((grad_middle + grad_layer).astype(jnp.bfloat16), term_qkv)


def local(tokens, ocean_count, w_qkv, w_out, w_up, w_down, cotangent):
    band_rows, local_len, model_width = tokens.shape
    head_count = model_width // HEAD_DIM
    ocean_mask = (lax.broadcasted_iota(jnp.int32, (band_rows, local_len), 1) < ocean_count).astype(
        jnp.float32
    )
    key_land_mask = ocean_mask.astype(jnp.bfloat16)
    normed, query_b, key_value, query_raw, key_raw = project_in(tokens, w_qkv, head_count)
    part_numerator, part_total = lax.map(
        lambda row_items: attend_row(row_items[0], row_items[1], row_items[2], head_count),
        (
            query_b,
            lax.all_gather(key_value, "lon", axis=1, tiled=True),
            lax.all_gather(key_land_mask, "lon", axis=1, tiled=True),
        ),
    )
    attended = (split_heads(part_numerator, head_count) / part_total[..., None]).reshape(
        band_rows, local_len, model_width
    )
    attended_b = attended.astype(jnp.bfloat16)
    block_out, tail_saved = forward_tail(tokens, attended_b, ocean_mask, w_out, w_up, w_down)
    grad_middle, grad_attended, tail_terms = backward_tail(
        cotangent, ocean_mask, attended_b, tail_saved, w_out, w_up, w_down
    )
    gradient_correction = jnp.sum(split_heads(widen(grad_attended) * attended, head_count), axis=-1)
    keys_all, masks_all = (
        lax.all_gather(key_value, "lon", axis=1, tiled=True),
        lax.all_gather(key_land_mask, "lon", axis=1, tiled=True),
    )
    grad_query, kv_terms = lax.map(
        lambda row_items: attend_row_back(
            row_items[0],
            row_items[1],
            row_items[2],
            row_items[3],
            row_items[4],
            row_items[5],
            head_count,
        ),
        (query_b, keys_all, masks_all, part_total, grad_attended, gradient_correction),
    )
    grad_kv = lax.psum_scatter(
        kv_terms.astype(jnp.bfloat16), "lon", scatter_dimension=1, tiled=True
    ).astype(jnp.float32)
    grad_tokens, term_qkv = backward_head(
        tokens, normed, query_raw, key_raw, grad_query, grad_kv, grad_middle, w_qkv, head_count
    )
    grad_scale = 1.0 / math.sqrt(
        band_rows * lax.axis_size("lat") * local_len * lax.axis_size("lon")
    )
    grad_terms = (
        term_qkv * grad_scale,
        tail_terms[0] * grad_scale,
        tail_terms[1] * grad_scale,
        tail_terms[2] * grad_scale,
    )
    band_parts = (
        lax.psum_scatter(grad_terms[0], "lat", scatter_dimension=0, tiled=True),
        lax.psum_scatter(grad_terms[1], "lat", scatter_dimension=0, tiled=True),
        lax.psum_scatter(grad_terms[2], "lat", scatter_dimension=0, tiled=True),
        lax.psum_scatter(grad_terms[3], "lat", scatter_dimension=0, tiled=True),
    )
    summed = (
        lax.psum(band_parts[0].astype(jnp.bfloat16), "lon").astype(jnp.float32),
        lax.psum(band_parts[1].astype(jnp.bfloat16), "lon").astype(jnp.float32),
        lax.psum(band_parts[2].astype(jnp.bfloat16), "lon").astype(jnp.float32),
        lax.psum(band_parts[3].astype(jnp.bfloat16), "lon").astype(jnp.float32),
    )
    return (block_out, grad_tokens, summed[0], summed[1], summed[2], summed[3])


def solution(mesh):
    in_specs = (P("lat", "lon", None), P("lat", "lon"), P(), P(), P(), P(), P("lat", "lon", None))
    out_specs = (
        P("lat", "lon", None),
        P("lat", "lon", None),
        P("lat", None),
        P("lat", None),
        P("lat", None),
        P("lat", None),
    )
    return jax.shard_map(local, mesh=mesh, in_specs=in_specs, out_specs=out_specs, check_vma=False)
```

profile of v0, /device:TPU:0, one launch (start us, length us, event | category | flops | bytes accessed | tf_op | source)
XLA Modules:
  0.0 455.0 jit_solution(4694651029376068034)
XLA Ops:
  7.2 1.1 convert_reduce_fusion
  8.4 1.1 fusion.49
  10.1 1.4 fusion.20
  13.3 1.2 mul.334
  17.1 1.2 mul.335
  18.3 1.3 mul.336
  20.7 1.4 reduce_sum.133
  22.3 1.2 mul.330
  23.5 1.3 mul.331
  27.5 6.0 %all-gather = bf16[4,64,3]{1,2,0:T(4,128)(2,1)S(1)} all-gather(bf16[1,64,3]{1,2,0:T(4,128)(2,1)S(1)} %get-tuple-element.344), channel_id=1, replica_groups=mesh['lat'=8,'lon'=4] {'lon'}, dimensions={0}, use_global_device_ids=true | all-gather | bytes 1920 | tf_op jit(solution)/shard_map/all_gather | solution.py:166
  33.6 15.7 %all-gather.3.cloned.1.call-done = bf16[3,256,1024]{2,1,0:T(8,128)(2,1)} async-done(((bf16[3,64,1024]{2,1,0:T(8,128)(2,1)}), bf16[3,256,1024]{2,1,0:T(8,128)(2,1)}) %all-gather.3.cloned.1.call-update) | async-done | bytes 1572880 | tf_op jit(solution)/shard_map/all_gather | solution.py:165
  49.3 2.6 copy.91
  52.0 8.6 %while.28 = (s32[]{:T(128)}, f32[3,64,512]{2,1,0:T(8,128)S(1)}, f32[3,64,8]{1,2,0:T(8,128)S(1)}, bf16[3,256,1024]{1,2,0:T(8,128)(2,1)}, bf16[3,64,512]{2,1,0:T(8...) while((s32[]{:T(128)}, f32[3,64,512]{2,1,0:T(8,128)S(1)}, f32[3,64,8]{1,2,0:T(8,128)S(1)}, ...), condition=%wide.region_6.7_spmd, body=%wide.region_4.6_spmd.sunk | while | flops 34209536 | bytes 4141673 | solution.py:161
  62.0 1.2 div.95
  64.3 1.1 div.97
  72.3 1.4 reduce_sum.142
  74.6 18.3 %while.29 = (s32[]{:T(128)}, f32[3,64,512]{2,1,0:T(8,128)}, bf16[3,256,1024]{2,1,0:T(8,128)(2,1)}, bf16[3,256,1024]{1,2,0:T(8,128)(2,1)}, bf16[3,64,512]{2,1,0:T...) while((s32[]{:T(128)}, f32[3,64,512]{2,1,0:T(8,128)}, ...), condition=%wide.region_13.14_spmd, body=%wide.region_12.13_spmd.sunk | while | flops 86114560 | bytes 10369669 | solution.py:182
  94.0 1.3 fusion.22
  95.4 1.9 bitcast_multiply_fusion.1
  98.5 1.9 bitcast_multiply_fusion
  101.8 1.8 slice_multiply_fusion
  103.7 2.1 mul.368
  105.7 1.4 reduce_sum.143
  107.3 1.2 broadcast_in_dim.80
  108.5 2.1 broadcast_in_dim.81
  110.6 10.6 %reduce-scatter.6.cloned.1.call-done = bf16[3,64,1024]{2,1,0:T(8,128)(2,1)} async-done(((bf16[3,256,1024]{2,1,0:T(8,128)(2,1)}), bf16[3,64,1024]{2,1,0:T(8,128)(2,1)}) %reduce-scatter.6.cloned.1.call-update) | async-done | bytes 393232 | tf_op jit(solution)/shard_map/reduce_scatter | solution.py:194
  121.3 2.3 fusion.52
  123.6 2.1 mul.374
  125.6 1.4 reduce_sum.147
  127.3 1.2 broadcast_in_dim.82
  128.4 2.1 broadcast_in_dim.83
  131.5 1.4 fusion.53
  133.6 2.3 fusion.17
  137.1 2.3 fusion.25
  139.4 49.0 %reduce-scatter.10.cloned.1.call-done = f32[64,512]{1,0:T(8,128)} async-done(((f32[512,512]{1,0:T(8,128)}), f32[64,512]{1,0:T(8,128)}) %reduce-scatter.10.cloned.1.call-update) | async-done | bytes 131088 | tf_op jit(solution)/shard_map/reduce_scatter | solution.py:211
  188.4 1.5 convert_element_type.147
  190.0 1.7 fusion.51
  191.9 66.7 %reduce-scatter.12.cloned.1.call-done = f32[64,1024]{1,0:T(8,128)} async-done(((f32[512,1024]{1,0:T(8,128)}), f32[64,1024]{1,0:T(8,128)}) %reduce-scatter.12.cloned.1.call-update) | async-done | bytes 262160 | tf_op jit(solution)/shard_map/reduce_scatter | solution.py:212
  258.7 1.6 convert_element_type.149
  260.3 68.6 %reduce-scatter.14.cloned.1.call-done = f32[128,512]{1,0:T(8,128)} async-done(((f32[1024,512]{1,0:T(8,128)}), f32[128,512]{1,0:T(8,128)}) %reduce-scatter.14.cloned.1.call-update) | async-done | bytes 262160 | tf_op jit(solution)/shard_map/reduce_scatter | solution.py:213
  328.9 1.6 convert_element_type.151
  330.5 75.4 %reduce-scatter.8.cloned.1.call-done = f32[64,1536]{1,0:T(8,128)} async-done(((f32[512,1536]{1,0:T(8,128)}), f32[64,1536]{1,0:T(8,128)}) %reduce-scatter.8.cloned.1.call-update) | async-done | bytes 393232 | tf_op jit(solution)/shard_map/reduce_scatter | solution.py:210
  405.9 1.7 convert_element_type.145
  408.6 33.1 %all-reduce.3.cloned.1.call-done = (bf16[64,1536]{1,0:T(8,128)(2,1)}, bf16[64,512]{1,0:T(8,128)(2,1)}, bf16[64,1024]{1,0:T(8,128)(2,1)}, bf16[128,512]{1,0:T(8,128)(2,1)}) async-done(((bf16[64,1536]{1,0:T(8,128)(2,1)}, bf16[64,512]{1,0:T(8,128)(2,1)}, bf16[64,1024]{1,0:T(8,128)(2,1)}, bf16[128,512]{1,0:T(8,128)(2,1)}), (bf16[64,1536]{1,0:T(8,128)(2,1)}, bf16[64,512]{1,0:T(8,128)(2,1)}, ...) | async-done | bytes 524304 | tf_op jit(solution)/shard_map/psum | solution.py:216
  441.7 1.5 convert_element_type.148
  443.2 1.7 convert_element_type.146
  444.9 1.6 convert_element_type.150
  446.5 1.6 convert_element_type.152
  (230 shorter events, 53.5 us)
Async XLA Ops:
  7.2 2.9 copy-start
  7.2 42.2 %all-gather.3.cloned.1.call-start = ((), (), s32[]{:S(2)}) async-start(), calls=%async_computation.5 | async-start | bytes 1966080 | tf_op jit(solution)/shard_map/all_gather | solution.py:165
  8.4 3.2 copy-start.34
  10.1 2.2 copy-start.36
  11.6 13.3 %copy-start.1 = (f32[3,64,1536]{2,1,0:T(8,128)}, f32[3,64,1536]{2,1,0:T(8,128)S(1)}, u32[]{:S(2)}) copy-start(f32[3,64,1536]{2,1,0:T(8,128)S(1)} %fusion.20) | copy-start | bytes 3538948
  15.4 4.3 copy-start.16
  19.6 32.3 %copy-start.10 = (f32[3,64,512]{2,1,0:T(8,128)}, f32[3,64,512]{2,1,0:T(8,128)S(1)}, u32[]{:S(2)}) copy-start(f32[3,64,512]{2,1,0:T(8,128)S(1)} %mul.336) | copy-start | bytes 1179652
  24.9 27.1 %copy-start.9 = (f32[3,64,512]{2,1,0:T(8,128)}, f32[3,64,512]{2,1,0:T(8,128)S(1)}, u32[]{:S(2)}) copy-start(f32[3,64,512]{2,1,0:T(8,128)S(1)} %mul.331) | copy-start | bytes 1179652
  24.9 1.1 copy-start.22
  24.9 2.0 copy-start.41
  26.8 94.4 %reduce-scatter.6.cloned.1.call-start = ((), (), s32[]{:S(2)}) async-start(), calls=%async_computation.6 | async-start | bytes 1966080 | tf_op jit(solution)/shard_map/reduce_scatter | solution.py:194
  60.5 0.7 copy-start.14
  60.5 0.7 copy-start.33
  62.0 2.2 copy-start.15
  62.0 3.4 copy-start.3
  62.0 3.4 copy-start.11
  62.0 3.4 copy-start.38
  64.3 1.8 copy-start.6
  65.4 4.8 %copy-start.4 = (f32[3,64,512]{2,1,0:T(8,128)}, f32[3,64,512]{2,1,0:T(8,128)S(1)}, u32[]{:S(2)}) copy-start(f32[3,64,512]{2,1,0:T(8,128)S(1)} %div.97) | copy-start | bytes 1179652
  65.8 0.9 copy-start.23
  65.8 1.3 copy-start.42
  67.1 0.9 copy-start.19
  68.0 0.8 copy-start.17
  69.0 3.2 copy-start.7
  69.2 1.0 copy-start.12
  92.9 1.0 copy-start.5
  92.9 1.0 copy-start.13
  93.0 2.4 copy-start.18
  93.0 95.5 %reduce-scatter.10.cloned.1.call-start = ((), (), s32[]{:S(2)}) async-start(), calls=%async_computation.8 | async-start | bytes 1179648 | tf_op jit(solution)/shard_map/reduce_scatter | solution.py:211
  95.3 163.3 %reduce-scatter.12.cloned.1.call-start = ((), (), s32[]{:S(2)}) async-start(), calls=%async_computation.9 | async-start | bytes 2359296 | tf_op jit(solution)/shard_map/reduce_scatter | solution.py:212
  97.3 1.2 copy-start.20
  97.3 1.2 copy-start.24
  97.4 231.5 %reduce-scatter.14.cloned.1.call-start = ((), (), s32[]{:S(2)}) async-start(), calls=%async_computation.10 | async-start | bytes 2359296 | tf_op jit(solution)/shard_map/reduce_scatter | solution.py:213
  100.5 1.4 copy-start.2
  100.5 305.5 %reduce-scatter.8.cloned.1.call-start = ((), (), s32[]{:S(2)}) async-start(), calls=%async_computation.7 | async-start | bytes 3538944 | tf_op jit(solution)/shard_map/reduce_scatter | solution.py:210
  101.8 5.4 %copy-start.32 = (f32[3,64,8]{1,2,0:T(8,128)S(1)}, f32[3,64,8]{1,2,0:T(8,128)}, u32[]{:S(2)}) copy-start(f32[3,64,8]{1,2,0:T(8,128)} %copy-done.31) | copy-start | bytes 18436
  128.4 5.2 %copy-start.35 = (f32[3,64]{1,0:T(4,128)S(1)}, f32[3,64]{1,0:T(4,128)}, u32[]{:S(2)}) copy-start(f32[3,64]{1,0:T(4,128)} %copy-done.34) | copy-start | bytes 2308
  128.4 5.2 %copy-start.37 = (f32[3,64]{1,0:T(4,128)S(1)}, f32[3,64]{1,0:T(4,128)}, u32[]{:S(2)}) copy-start(f32[3,64]{1,0:T(4,128)} %copy-done.36) | copy-start | bytes 2308
  130.5 3.1 copy-start.30
  131.5 1.4 copy-start.28
  132.9 0.7 copy-start.26
  136.0 1.1 copy-start.21
  136.0 54.0 %copy-start.27 = (bf16[3,64,512]{2,1,0:T(8,128)(2,1)S(1)}, bf16[3,64,512]{2,1,0:T(8,128)(2,1)}, u32[]{:S(2)}) copy-start(bf16[3,64,512]{2,1,0:T(8,128)(2,1)} %copy-done.26) | copy-start | bytes 589828
  136.0 54.0 %copy-start.29 = (bf16[3,64,512]{2,1,0:T(8,128)(2,1)S(1)}, bf16[3,64,512]{2,1,0:T(8,128)(2,1)}, u32[]{:S(2)}) copy-start(bf16[3,64,512]{2,1,0:T(8,128)(2,1)} %copy-done.28) | copy-start | bytes 589828
  136.0 305.7 %all-reduce.3.cloned.1.call-start = ((), (), s32[]{:S(2)}) async-start(), calls=%async_computation.11 | async-start | bytes 1048576 | tf_op jit(solution)/shard_map/psum | solution.py:216
  190.0 1.7 copy-start.40
  191.7 216.0 %copy-start.8 = (f32[3,64,512]{2,1,0:T(8,128)S(1)}, f32[3,64,512]{2,1,0:T(8,128)}, u32[]{:S(2)}) copy-start(f32[3,64,512]{2,1,0:T(8,128)} %copy-done.7) | copy-start | bytes 1179652
  191.7 216.0 %copy-start.25 = (bf16[3,64,512]{2,1,0:T(8,128)(2,1)S(1)}, bf16[3,64,512]{2,1,0:T(8,128)(2,1)}, u32[]{:S(2)}) copy-start(bf16[3,64,512]{2,1,0:T(8,128)(2,1)} %param.17) | copy-start | bytes 589828
  (2 other events, 1.2 us)
Sparse Core Ops, SparseCore 0:
  26.9 22.3 all-gather.2
  93.1 28.1 reduce-scatter.5
  125.1 63.3 reduce-scatter.9
  191.8 66.8 reduce-scatter.11
  262.1 66.7 reduce-scatter.13
  332.3 73.5 reduce-scatter.7
  409.1 32.5 all-reduce.2
where the time goes:
time: 457 us; the launch traced here: 455 us
  waiting for transfers between devices  319 us (70%)
  local copies, waits for them, and re-layouts  58 us (13%)
  other arithmetic  34.6 us (8%)
  matrix products  21.5 us (5%)
  between operations  14.7 us (3%)
  blocking collectives  5.97 us (1%)
    reduce_scatter x1, waiting for transfers between devices, local(): lax.psum_scatter(grad_terms[0], 'lat', scatter_dimension=0, tiled=True)  75.4 us
    reduce_scatter x1, waiting for transfers between devices, local(): lax.psum_scatter(grad_terms[3], 'lat', scatter_dimension=0, tiled=True)  68.6 us
    reduce_scatter x1, waiting for transfers between devices, local(): lax.psum_scatter(grad_terms[2], 'lat', scatter_dimension=0, tiled=True)  66.7 us
    reduce_scatter x1, waiting for transfers between devices, local(): lax.psum_scatter(grad_terms[1], 'lat', scatter_dimension=0, tiled=True)  49 us
    psum x1, waiting for transfers between devices, local(): lax.psum(band_parts[0].astype(jnp.bfloat16), 'lon').astype(jnp.float32)  33.1 us
    dot_general x33, matrix products, elementwise_product(): jnp.einsum(pattern, left_side, right_side, preferred_element_type=jnp.flo...  21.5 us
    all_gather x1, waiting for transfers between devices, local(): lax.all_gather(key_value, 'lon', axis=1, tiled=True)  15.7 us
    reduce_scatter x1, waiting for transfers between devices, local(): lax.psum_scatter(kv_terms.astype(jnp.bfloat16), 'lon', scatter_dimension=...  10.6 us
  transfers between devices with their start and end apart: 7, of which 7 were waited for; matrix products, arithmetic and copies ran while one was open for 8% of the time, Pallas kernels for 0%

commit v1 on v0

v1 whole, which is shorter than its diff:
```python
import functools
import math

import jax
import jax.numpy as jnp
from jax import lax
from jax.experimental import pallas as pl
from jax.experimental.pallas import tpu as pltpu
from jax.sharding import PartitionSpec as P

HEAD_DIM = 64
SECTORS = 4
QUAD = 4 * HEAD_DIM
LANES = 128
MESH = pl.DeviceIdType.MESH
F32 = jnp.float32
BF16 = jnp.bfloat16


def nn(a, b):
    return jnp.dot(a, b, preferred_element_type=F32)


def nt(a, b):
    return lax.dot_general(a, b, (((1,), (1,)), ((), ())), preferred_element_type=F32)


def tn(a, b):
    return lax.dot_general(a, b, (((0,), (0,)), ((), ())), preferred_element_type=F32)


def split_two(values):
    high = values.astype(BF16)
    return high, (values - high.astype(F32)).astype(BF16)


def norm_stats(values):
    average = jnp.mean(values, axis=-1, keepdims=True)
    centered = values - average
    variance = jnp.mean(centered * centered, axis=-1, keepdims=True)
    inverse = lax.rsqrt(variance + 1e-05)
    return centered * inverse, inverse


def norm_back(grad, normed, inverse):
    first = jnp.mean(grad, axis=-1, keepdims=True)
    second = jnp.mean(grad * normed, axis=-1, keepdims=True)
    return inverse * (grad - first - normed * second)


def head_mean(values, blocks):
    parts = []
    for start in range(0, values.shape[1], QUAD):
        high, low = split_two(values[:, start : start + QUAD])
        parts.append(nn(high, blocks) + nn(low, blocks))
    return jnp.concatenate(parts, axis=1)


def kernel(lat_n, scale, *refs):
    x_ref, cot_ref, wqkv, wout, wup, wdown = refs[:6]
    bo_ref, gt_ref, gqkv, gout, gup, gdown = refs[6:12]
    xg, ka, va, ma, qa, probs, att_ref, ivb_ref, dq_ref, dk_ref, dv_ref, gaall, stats = refs[12:25]
    own_sem_s, own_sem_r, lat_s, lat_r, all_s, all_r = refs[25:31]
    bufs = refs[31:]
    rows, length, wide = x_ref.shape
    width = wide - LANES
    count = rows * length
    quads = width // QUAD

    lat = lax.axis_index("lat")
    lon = lax.axis_index("lon")
    x_pos, core = lon // 2, lon % 2
    core_peer = (lat, x_pos * 2 + (1 - core))
    x_peer = (lat, (1 - x_pos) * 2 + core)
    far_peer = (lat, (1 - x_pos) * 2 + (1 - core))

    barrier = pltpu.get_barrier_semaphore()
    for peer in (core_peer, x_peer, far_peer):
        pl.semaphore_signal(barrier, inc=1, device_id=peer, device_id_type=MESH)

    @pl.loop(1, lat_n)
    def _(offset):
        pl.semaphore_signal(
            barrier, inc=1, device_id=(lax.rem(lat + offset, lat_n), lon), device_id_type=MESH
        )

    pl.semaphore_wait(barrier, 3 + lat_n - 1)

    def remote(src, dst, send, recv, peer):
        return pltpu.make_async_remote_copy(
            src_ref=src, dst_ref=dst, send_sem=send, recv_sem=recv,
            device_id=peer, device_id_type=MESH,
        )

    def gather(src, buf, base):
        near = remote(src, buf.at[1], own_sem_s.at[base], own_sem_r.at[base], core_peer)
        across = remote(src, buf.at[2], own_sem_s.at[base + 1], own_sem_r.at[base + 1], x_peer)
        onward = remote(
            buf.at[2], buf.at[3], own_sem_s.at[base + 2], own_sem_r.at[base + 2], core_peer
        )
        across.start()
        near.start()
        return near, across, onward

    x_near, x_across, x_onward = gather(x_ref, xg, 0)

    lane = lax.broadcasted_iota(jnp.int32, (1, QUAD), 1) // HEAD_DIM
    lane_f = [jnp.where(lane == h, 1.0, 0.0).astype(F32) for h in range(4)]
    lane_b = [m.astype(BF16) for m in lane_f]
    blocks = jnp.where(
        lax.broadcasted_iota(jnp.int32, (QUAD, QUAD), 0) // HEAD_DIM
        == lax.broadcasted_iota(jnp.int32, (QUAD, QUAD), 1) // HEAD_DIM,
        1.0 / HEAD_DIM,
        0.0,
    ).astype(BF16)
    heads = width // HEAD_DIM
    head_row = lax.broadcasted_iota(jnp.int32, (heads, width), 0)
    head_col = lax.broadcasted_iota(jnp.int32, (heads, width), 1)
    pick_sum = jnp.where(head_col // HEAD_DIM == head_row, 1.0, 0.0).astype(BF16)
    pick_one = jnp.where(head_col == head_row * HEAD_DIM, 1.0, 0.0).astype(BF16)

    def stack(tile):
        return jnp.concatenate([tile * lane_b[h] for h in range(4)], axis=0)

    def combine(tile):
        total = tile[:HEAD_DIM] * lane_f[0]
        for h in range(1, 4):
            total = total + tile[h * length : (h + 1) * length] * lane_f[h]
        return total

    def per_row(values):
        return values.reshape(rows, length, values.shape[-1])

    def project(slot):
        block = (x_ref[...] if slot == 0 else xg[slot]).reshape(count, wide)
        mask = block[:, width:]
        mask_wide = jnp.concatenate([mask.astype(F32)] * (width // LANES), axis=1)
        normed, inverse = norm_stats(block[:, :width].astype(F32))
        normed_b = normed.astype(BF16)
        query_raw = nn(normed_b, wqkv[:, :width])
        key_raw = nn(normed_b, wqkv[:, width : 2 * width])
        value = nn(normed_b, wqkv[:, 2 * width :])
        q_inv = lax.rsqrt(head_mean(query_raw * query_raw, blocks) + 1e-06)
        k_inv = lax.rsqrt(head_mean(key_raw * key_raw, blocks) + 1e-06)
        at = pl.ds(slot * length, length)
        qa[:, at, :] = per_row((query_raw * q_inv).astype(BF16))
        ka[:, at, :] = per_row((key_raw * k_inv * mask_wide).astype(BF16))
        va[:, at, :] = per_row((value * mask_wide).astype(BF16))
        ma[:, at, :] = per_row(mask)
        return normed, inverse, normed_b, query_raw, key_raw, q_inv, k_inv, mask_wide

    normed, inverse, normed_b, query_raw, key_raw, q_inv, k_inv, mask_wide = project(0)
    x_near.wait_recv()
    project(1)
    x_across.wait_recv()
    x_onward.start()
    project(2)
    x_onward.wait_recv()
    project(3)
    for copy in (x_near, x_across, x_onward):
        copy.wait_send()

    logit = 8.0 / HEAD_DIM

    @pl.loop(0, rows)
    def _(r):
        for qd in range(quads):
            cs = slice(qd * QUAD, (qd + 1) * QUAD)
            key, value = ka[r, :, cs], va[r, :, cs]
            score = jnp.exp(nt(stack(qa[r, 0:length, cs]), key) * logit - 8.0)
            score_b = score.astype(BF16)
            part = 1.0 / nn(score_b, ma[r])
            part = jnp.concatenate([part, part], axis=1)
            probs[r, qd] = score * part
            att_ref[r, :, cs] = combine(nn(score_b, value) * part)
            ivb_ref[r, :, cs] = combine(part)

    tokens = x_ref[...].reshape(count, wide)[:, :width].astype(F32)
    cotangent = cot_ref[...].reshape(count, width).astype(F32)
    attended = att_ref[...].reshape(count, width)
    attended_b = attended.astype(BF16)
    middle = tokens + mask_wide * nn(attended_b, wout[...])
    normed_two, inverse_two = norm_stats(middle)
    normed_two_b = normed_two.astype(BF16)
    lifted = nn(normed_two_b, wup[...])
    root = math.sqrt(2.0 / math.pi)
    square = lifted * lifted
    curve = jnp.tanh(root * lifted * (1.0 + 0.044715 * square))
    half = 0.5 * (1.0 + curve)
    active = (lifted * half).astype(BF16)
    slope = half + 0.5 * lifted * (1.0 - curve * curve) * (root * (1.0 + 3 * 0.044715 * square))
    bo_ref[...] = per_row((middle + mask_wide * nn(active, wdown[...])).astype(BF16))

    grad_branch = (mask_wide * cotangent).astype(BF16)
    grad_lifted = (slope * nt(grad_branch, wdown[...])).astype(BF16)
    grad_middle = cotangent + norm_back(nt(grad_lifted, wup[...]), normed_two, inverse_two)
    grad_attn = (mask_wide * grad_middle).astype(BF16)
    grad_attended = nt(grad_attn, wout[...]).astype(BF16)
    gaall[0] = per_row(grad_attended)
    product = per_row(grad_attended.astype(F32) * attended)
    for r in range(rows):
        high, low = split_two(ivb_ref[r])
        part = nt(pick_one, high) + nt(pick_one, low)
        high, low = split_two(product[r])
        delta = nt(pick_sum, high) + nt(pick_sum, low)
        pair = jnp.concatenate([part, delta], axis=0)
        stats[0, r] = jnp.concatenate([pair, jnp.zeros_like(pair)], axis=1)

    g_near, g_across, g_onward = gather(gaall.at[0], gaall, 3)
    s_near, s_across, s_onward = gather(stats.at[0], stats, 6)

    pending = {}

    def begin(c, left, right):
        part, from_core, to_x, from_x, total, from_lat, mine, everyone = bufs[8 * c : 8 * c + 8]
        _, _, n, r, c4 = part.shape
        full = tn(left, right) * scale
        for l in range(SECTORS):
            part[l % 2, l // 2] = full[:, l * c4 : (l + 1) * c4].reshape(n, r, c4).astype(BF16)
        base = 9 + 5 * c
        copy = remote(
            part.at[1 - core], from_core, own_sem_s.at[base], own_sem_r.at[base], core_peer
        )
        copy.start()
        pending[c] = copy

    def pass_x(c):
        part, from_core, to_x, from_x, total, from_lat, mine, everyone = bufs[8 * c : 8 * c + 8]
        pending[c].wait()
        other = 1 - x_pos
        to_x[...] = (
            part[core, other].astype(F32) + from_core[other].astype(F32)
        ).astype(BF16)
        base = 9 + 5 * c + 1
        copy = remote(to_x, from_x, own_sem_s.at[base], own_sem_r.at[base], x_peer)
        copy.start()
        pending[c] = copy

    def lat_copy(c, offset):
        total, from_lat = bufs[8 * c + 4], bufs[8 * c + 5]
        target = lax.rem(lat + offset, lat_n)
        return remote(
            total.at[target], from_lat.at[offset - 1],
            lat_s.at[c, offset - 1], lat_r.at[c, offset - 1], (target, lon),
        )

    def pass_lat(c):
        part, from_core, to_x, from_x, total, from_lat, mine, everyone = bufs[8 * c : 8 * c + 8]
        pending[c].wait()
        total[...] = (
            part[core, x_pos].astype(F32) + from_core[x_pos].astype(F32) + from_x[...].astype(F32)
        ).astype(BF16)

        @pl.loop(1, lat_n)
        def _(offset):
            lat_copy(c, offset).start()

    def pass_lon(c):
        part, from_core, to_x, from_x, total, from_lat, mine, everyone = bufs[8 * c : 8 * c + 8]

        @pl.loop(1, lat_n)
        def _(offset):
            lat_copy(c, offset).wait()

        everyone[lon] = (
            total[lat].astype(F32) + jnp.sum(from_lat[...].astype(F32), axis=0)
        ).astype(BF16)
        copies = []
        for i, peer in enumerate((x_peer, far_peer, core_peer)):
            copy = remote(
                everyone.at[lon], everyone.at[lon], all_s.at[c, i], all_r.at[c, i], peer
            )
            copy.start()
            copies.append(copy)
        pending[c] = copies

    def finish(c, out, first):
        everyone = bufs[8 * c + 7]
        c4 = everyone.shape[-1]
        for copy in pending[c]:
            copy.wait()
        for l in range(SECTORS):
            out[:, first + l * c4 : first + (l + 1) * c4] = everyone[l].astype(F32)

    begin(0, active, grad_branch)
    begin(1, normed_two_b, grad_lifted)
    pass_x(0)
    begin(2, attended_b, grad_attn)

    @pl.loop(0, rows)
    def _(r):
        for qd in range(quads):
            cs = slice(qd * QUAD, (qd + 1) * QUAD)
            key, value = ka[r, :, cs], va[r, :, cs]
            tall = stack(gaall[0, r, :, cs])
            delta = jnp.sum(
                tall.astype(F32) * jnp.concatenate([att_ref[r, :, cs]] * 4, axis=0),
                axis=-1,
                keepdims=True,
            )
            back = (probs[r, qd] * (nt(tall, value) - delta) * logit).astype(BF16)
            dq_ref[r, :, cs] = combine(nn(back, key))

    def head_back(grad, raw, inv):
        return inv * (grad - raw * (inv * inv) * head_mean(raw * grad, blocks))

    g_across.wait_recv()
    g_onward.start()
    s_across.wait_recv()
    s_onward.start()
    pass_x(1)
    grad_q = head_back(dq_ref[...].reshape(count, width), query_raw, q_inv).astype(BF16)
    begin(3, normed_b, grad_q)
    pass_x(2)
    pass_lat(0)
    for copy in (g_near, s_near, g_onward, s_onward):
        copy.wait_recv()

    @pl.loop(0, rows)
    def _(r):
        stat = jnp.concatenate([stats[s, r][:, :length] for s in range(SECTORS)], axis=1)
        for qd in range(quads):
            cs = slice(qd * QUAD, (qd + 1) * QUAD)
            query = qa[r, :, cs]
            grad = jnp.concatenate([gaall[s, r, :, cs] for s in range(SECTORS)], axis=0)

            def spread(base):
                return jnp.concatenate(
                    [
                        jnp.broadcast_to(stat[base + h : base + h + 1], (length, QUAD))
                        for h in range(qd * 4, qd * 4 + 4)
                    ],
                    axis=0,
                )

            score = jnp.exp(nt(stack(ka[r, 0:length, cs]), query) * logit - 8.0) * spread(0)
            deep = nt(stack(va[r, 0:length, cs]), grad)
            back = (score * (deep - spread(heads)) * logit).astype(BF16)
            dk_ref[r, :, cs] = combine(nn(back, query))
            dv_ref[r, :, cs] = combine(nn(score.astype(BF16), grad))

    pass_x(3)
    pass_lat(1)
    grad_k = head_back(
        dk_ref[...].reshape(count, width) * mask_wide, key_raw, k_inv
    ).astype(BF16)
    grad_v = (dv_ref[...].reshape(count, width) * mask_wide).astype(BF16)
    grad_kv = jnp.concatenate([grad_k, grad_v], axis=1)
    begin(4, normed_b, grad_kv)
    pass_lat(2)
    pass_lon(0)
    pass_x(4)
    grad_normed = (
        nt(grad_q, wqkv[:, :width])
        + nt(grad_k, wqkv[:, width : 2 * width])
        + nt(grad_v, wqkv[:, 2 * width :])
    )
    gt_ref[...] = per_row((grad_middle + norm_back(grad_normed, normed, inverse)).astype(BF16))
    pass_lat(3)
    pass_lon(1)
    finish(0, gdown, 0)
    pass_lon(2)
    finish(1, gup, 0)
    pass_lat(4)
    pass_lon(3)
    finish(2, gout, 0)
    finish(3, gqkv, 0)
    for copy in (g_near, g_across, g_onward, s_near, s_across, s_onward):
        copy.wait_send()
    pass_lon(4)
    finish(4, gqkv, width)


def local(lat_n, tokens, ocean_count, w_qkv, w_out, w_up, w_down, cotangent):
    rows, length, width = tokens.shape
    heads = width // HEAD_DIM
    hidden = w_up.shape[1]
    lon_n = SECTORS
    mask = (
        lax.broadcasted_iota(jnp.int32, (rows, length, LANES), 1) < ocean_count[:, :, None]
    ).astype(BF16)
    extended = jnp.concatenate([tokens, mask], axis=-1)
    scale = 1.0 / math.sqrt(rows * lat_n * length * lon_n)
    quads = width // QUAD
    full = length * SECTORS
    scratch = [
        pltpu.VMEM((SECTORS, rows, length, width + LANES), BF16),
        pltpu.VMEM((rows, full, width), BF16),
        pltpu.VMEM((rows, full, width), BF16),
        pltpu.VMEM((rows, full, LANES), BF16),
        pltpu.VMEM((rows, full, width), BF16),
        pltpu.VMEM((rows, quads, 4 * length, full), F32),
        pltpu.VMEM((rows, length, width), F32),
        pltpu.VMEM((rows, length, width), F32),
        pltpu.VMEM((rows, length, width), F32),
        pltpu.VMEM((rows, length, width), F32),
        pltpu.VMEM((rows, length, width), F32),
        pltpu.VMEM((SECTORS, rows, length, width), BF16),
        pltpu.VMEM((SECTORS, rows, 2 * heads, LANES), F32),
        pltpu.SemaphoreType.DMA((34,)),
        pltpu.SemaphoreType.DMA((34,)),
        pltpu.SemaphoreType.DMA((5, lat_n - 1)),
        pltpu.SemaphoreType.DMA((5, lat_n - 1)),
        pltpu.SemaphoreType.DMA((5, 3)),
        pltpu.SemaphoreType.DMA((5, 3)),
    ]
    for tall, broad in (
        (hidden, width), (width, hidden), (width, width), (width, width), (width, 2 * width)
    ):
        r, c4 = tall // lat_n, broad // SECTORS
        scratch += [
            pltpu.VMEM((2, 2, lat_n, r, c4), BF16),
            pltpu.VMEM((2, lat_n, r, c4), BF16),
            pltpu.VMEM((lat_n, r, c4), BF16),
            pltpu.VMEM((lat_n, r, c4), BF16),
            pltpu.VMEM((lat_n, r, c4), BF16),
            pltpu.VMEM((lat_n - 1, r, c4), BF16),
            pltpu.VMEM((8, LANES), BF16),
            pltpu.VMEM((SECTORS, r, c4), BF16),
        ]
    vmem = pl.BlockSpec(memory_space=pltpu.VMEM)
    return pl.pallas_call(
        functools.partial(kernel, lat_n, scale),
        out_shape=(
            jax.ShapeDtypeStruct(tokens.shape, BF16),
            jax.ShapeDtypeStruct(tokens.shape, BF16),
            jax.ShapeDtypeStruct((width // lat_n, 3 * width), F32),
            jax.ShapeDtypeStruct((width // lat_n, width), F32),
            jax.ShapeDtypeStruct((width // lat_n, hidden), F32),
            jax.ShapeDtypeStruct((hidden // lat_n, width), F32),
        ),
        in_specs=[vmem] * 6,
        out_specs=(vmem,) * 6,
        scratch_shapes=scratch,
        compiler_params=pltpu.CompilerParams(
            collective_id=0, has_side_effects=True, vmem_limit_bytes=56 * 1024 * 1024
        ),
    )(extended, cotangent, w_qkv, w_out, w_up, w_down)


def solution(mesh):
    rows = P("lat", "lon", None)
    in_specs = (rows, P("lat", "lon"), P(), P(), P(), P(), rows)
    out_specs = (rows, rows, P("lat", None), P("lat", None), P("lat", None), P("lat", None))
    return jax.shard_map(
        functools.partial(local, mesh.shape["lat"]),
        mesh=mesh,
        in_specs=in_specs,
        out_specs=out_specs,
        check_vma=False,
    )
```

time: 457 us -> 75.8 us (0.17)
  waiting for transfers between devices: 319 us -> 0 us
  Pallas kernels: 0 us -> 65.4 us
  local copies, waits for them, and re-layouts: 58 us -> 7.14 us
  other arithmetic: 34.6 us -> 2.38 us
  matrix products: 21.5 us -> 0 us
  between operations: 14.7 us -> 0.67 us
  blocking collectives: 5.97 us -> 0 us
    reduce_scatter x5 -> x0, waiting for transfers between devices: 270 us -> none  [the longest x1 75.4 us: local(): lax.psum_scatter(grad_terms[0], 'lat', scatter_dimension=0, tiled=True)]
    pallas_call x0 -> x1, Pallas kernels: none -> 65.4 us  [local(): pl.pallas_call(functools.partial(kernel, lat_n, scale), out_shape=(jax.Sh...]
    psum x1 -> x0, waiting for transfers between devices: 33.1 us -> none  [local(): lax.psum(band_parts[0].astype(jnp.bfloat16), 'lon').astype(jnp.float32)]
    dot_general x33 -> x0, matrix products: 21.5 us -> none  [elementwise_product(): jnp.einsum(pattern, left_side, right_side, preferred_element_type=jnp.flo...]
    all_gather x1 -> x0, waiting for transfers between devices: 15.7 us -> none  [local(): lax.all_gather(key_value, 'lon', axis=1, tiled=True)]
    convert_element_type x17 -> x1, other arithmetic: 14.8 us -> 0.74 us  [local(): mask = (lax.broadcasted_iota(jnp.int32, (rows, length, LANES), 1) < ocean...]
    mul x8 -> x0, local copies, waits for them, and re-layouts: 11.4 us -> none  [the longest x6 9.14 us: head_norm(): shaped * lax.rsqrt(jnp.mean(shaped * shaped, axis=-1, keepdims=True) + 1e...]
    reduce_sum x10 -> x0, other arithmetic: 9.47 us -> none  [the longest x2 2.82 us: head_norm(): shaped * lax.rsqrt(jnp.mean(shaped * shaped, axis=-1, keepdims=True) + 1e...]
  transfers between devices with their start and end apart: 7 -> 0, of which waited for: 7 -> 0; matrix products, arithmetic and copies ran while one was open for 8% -> 0% of each run, Pallas kernels for 0% -> 0%
where the time goes in v1:
time: 75.8 us; the launch traced here: 75.6 us
  Pallas kernels  65.4 us (86%)
  local copies, waits for them, and re-layouts  7.14 us (9%)
  other arithmetic  2.38 us (3%)
    pallas_call x1, Pallas kernels, local(): pl.pallas_call(functools.partial(kernel, lat_n, scale), out_shape=(jax.Sh...  65.4 us
    unnamed x12, local copies, waits for them, and re-layouts  7.14 us
    concatenate x1, other arithmetic, local(): extended = jnp.concatenate([tokens, mask], axis=-1)  1.65 us

profile of v1, /device:TPU:0, one launch (start us, length us, event | category | flops | bytes accessed | tf_op | source)
XLA Modules:
  0.0 75.6 jit_solution(1064991079752487071)
XLA Ops:
  0.6 0.7 fusion
  1.4 1.6 %pad_maximum_fusion.refs_0_ = bf16[3,64,640]{2,1,0:T(8,128)(2,1)} fusion(bf16[3,64,128]{2,1,0:T(8,128)(2,1)S(1)} %fusion, bf16[3,64,512]{2,1,0:T(8,128)(2,1)} %param.7), kind=kLoop, calls=%fused_computation | loop fusion | flops 491520 | bytes 491520 | tf_op jit(solution)/shard_map/concatenate | solution.py:382
  3.0 65.4 %shard_map.118 = (bf16[3,64,512]{2,1,0:T(8,128)(2,1)}, bf16[3,64,512]{2,1,0:T(8,128)(2,1)}, f32[64,1536]{1,0:T(8,128)}, f32[64,512]{1,0:T(8,128)}, f32[64,1024]{1,0:T(8,128)}, /*index=5*/f32[128,512]{1,0:T(8,128)}) custom-call(bf16[3,64,640]{2,1,0:T(8,128)(2,1)} %pad_maximum_fusion.refs_0_, bf16[3,64,512]{2,1,0:T(8,128)(2,1)} %refs_1_.1, ...), custom_call_target="tpu_custom_call" | custom-call | tf_op jit(solution)/shard_map/pallas_call | solution.py:422
  68.4 0.0 copy-start.2
  68.4 0.0 copy-start.1
  68.4 0.0 copy-start
  68.4 1.7 %copy.19 = bf16[3,64,512]{2,1,0:T(8,128)(2,1)} copy(bf16[3,64,512]{2,1,0:T(8,128)(2,1)} %get-tuple-element.12) | data formatting | bytes 393216
  70.1 1.6 %copy.20 = bf16[3,64,512]{2,1,0:T(8,128)(2,1)} copy(bf16[3,64,512]{2,1,0:T(8,128)(2,1)} %get-tuple-element.13) | data formatting | bytes 393216
  71.7 1.8 %copy.21 = f32[64,1536]{1,0:T(8,128)} copy(f32[64,1536]{1,0:T(8,128)} %get-tuple-element.14) | data formatting | bytes 786432
  73.5 0.0 copy-done.2
  73.5 0.7 copy.22
  74.2 0.0 copy-done.1
  74.2 0.7 copy.23
  74.9 0.0 copy-done
  74.9 0.7 copy.24
Async XLA Ops:
  68.4 5.1 %copy-start.2 = (f32[64,512]{1,0:T(8,128)S(1)}, f32[64,512]{1,0:T(8,128)}, u32[]{:S(2)}) copy-start(f32[64,512]{1,0:T(8,128)} %get-tuple-element.15) | copy-start | bytes 393220
  68.4 5.7 %copy-start.1 = (f32[64,1024]{1,0:T(8,128)S(1)}, f32[64,1024]{1,0:T(8,128)}, u32[]{:S(2)}) copy-start(f32[64,1024]{1,0:T(8,128)} %get-tuple-element.16) | copy-start | bytes 786436
  68.4 6.4 %copy-start = (f32[128,512]{1,0:T(8,128)S(1)}, f32[128,512]{1,0:T(8,128)}, u32[]{:S(2)}) copy-start(f32[128,512]{1,0:T(8,128)} %get-tuple-element.17) | copy-start | bytes 786436

commit v2 on v1

v2 whole, which is shorter than its diff:
```python
import functools
import math

import jax
import jax.numpy as jnp
from jax import lax
from jax.experimental import pallas as pl
from jax.experimental.pallas import tpu as pltpu
from jax.sharding import PartitionSpec as P

HEAD_DIM = 64
SECTORS = 4
QUAD = 4 * HEAD_DIM
LANES = 128
MESH = pl.DeviceIdType.MESH
F32 = jnp.float32
BF16 = jnp.bfloat16


def nn(a, b):
    return jnp.dot(a, b, preferred_element_type=F32)


def nt(a, b):
    return lax.dot_general(a, b, (((1,), (1,)), ((), ())), preferred_element_type=F32)


def tn(a, b):
    return lax.dot_general(a, b, (((0,), (0,)), ((), ())), preferred_element_type=F32)


def split_two(values):
    high = values.astype(BF16)
    return high, (values - high.astype(F32)).astype(BF16)


def norm_stats(values):
    average = jnp.mean(values, axis=-1, keepdims=True)
    centered = values - average
    variance = jnp.mean(centered * centered, axis=-1, keepdims=True)
    inverse = lax.rsqrt(variance + 1e-05)
    return centered * inverse, inverse


def norm_back(grad, normed, inverse):
    first = jnp.mean(grad, axis=-1, keepdims=True)
    second = jnp.mean(grad * normed, axis=-1, keepdims=True)
    return inverse * (grad - first - normed * second)


def head_mean(values, blocks):
    parts = []
    for start in range(0, values.shape[1], QUAD):
        high, low = split_two(values[:, start : start + QUAD])
        parts.append(nn(high, blocks) + nn(low, blocks))
    return jnp.concatenate(parts, axis=1)


def kernel(lat_n, scale, *refs):
    x_ref, count_ref, cot_hbm, wqkv_hbm, wout_hbm, wup_hbm, wdown_hbm = refs[:7]
    bo_hbm, gt_hbm, gqkv_hbm, gout_hbm, gup_hbm, gdown_hbm = refs[7:13]
    cot_ref, wqkv, wout, wup, wdown = refs[13:18]
    bo_ref, gt_ref, gqkv, gout, gup, gdown = refs[18:24]
    xg, cg, ka, va, ma, qa, probs, att_ref, ivb_ref, dq_ref, dk_ref, dv_ref, gaall, stats = refs[24:38]
    sem_s, sem_r, lat_s, lat_r, all_s, all_r, in_sem, out_sem = refs[38:46]
    bufs = refs[46:]
    rows, length, width = x_ref.shape
    count = rows * length
    quads = width // QUAD
    half_n = lat_n // 2

    lat = lax.axis_index("lat")
    lon = lax.axis_index("lon")
    x_pos, core = lon // 2, lon % 2
    hi, lo = lat // 2, lat % 2
    core_peer = (lat, x_pos * 2 + (1 - core))
    x_peer = (lat, (1 - x_pos) * 2 + core)
    far_peer = (lat, (1 - x_pos) * 2 + (1 - core))
    lo_peer = (hi * 2 + (1 - lo), lon)

    barrier = pltpu.get_barrier_semaphore()
    for peer in (core_peer, x_peer, far_peer, lo_peer):
        pl.semaphore_signal(barrier, inc=1, device_id=peer, device_id_type=MESH)

    def hi_peer(offset):
        return lax.rem(hi + offset, half_n)

    @pl.loop(1, half_n)
    def _(offset):
        pl.semaphore_signal(
            barrier, inc=1, device_id=(hi_peer(offset) * 2 + lo, lon), device_id_type=MESH
        )

    loads = []
    for i, (src, dst) in enumerate(
        ((wqkv_hbm, wqkv), (wout_hbm, wout), (cot_hbm, cot_ref), (wup_hbm, wup), (wdown_hbm, wdown))
    ):
        load = pltpu.make_async_copy(src, dst, in_sem.at[i])
        load.start()
        loads.append(load)

    cg[0] = jnp.zeros_like(cg[0])
    cg[0, 0:rows] = jnp.broadcast_to(count_ref[...], (rows, LANES))
    pl.semaphore_wait(barrier, 4 + half_n - 1)

    def remote(src, dst, send, recv, peer):
        return pltpu.make_async_remote_copy(
            src_ref=src, dst_ref=dst, send_sem=send, recv_sem=recv,
            device_id=peer, device_id_type=MESH,
        )

    def gather(src, buf, base):
        near = remote(src, buf.at[1], sem_s.at[base], sem_r.at[base], core_peer)
        across = remote(src, buf.at[2], sem_s.at[base + 1], sem_r.at[base + 1], x_peer)
        onward = remote(buf.at[2], buf.at[3], sem_s.at[base + 2], sem_r.at[base + 2], core_peer)
        across.start()
        near.start()
        return near, across, onward

    c_near, c_across, c_onward = gather(cg.at[0], cg, 9)
    x_near, x_across, x_onward = gather(x_ref, xg, 0)

    lane = lax.broadcasted_iota(jnp.int32, (1, QUAD), 1) // HEAD_DIM
    lane_f = [jnp.where(lane == h, 1.0, 0.0).astype(F32) for h in range(4)]
    lane_b = [m.astype(BF16) for m in lane_f]
    blocks = jnp.where(
        lax.broadcasted_iota(jnp.int32, (QUAD, QUAD), 0) // HEAD_DIM
        == lax.broadcasted_iota(jnp.int32, (QUAD, QUAD), 1) // HEAD_DIM,
        1.0 / HEAD_DIM,
        0.0,
    ).astype(BF16)
    heads = width // HEAD_DIM
    head_row = lax.broadcasted_iota(jnp.int32, (heads, width), 0)
    head_col = lax.broadcasted_iota(jnp.int32, (heads, width), 1)
    pick_sum = jnp.where(head_col // HEAD_DIM == head_row, 1.0, 0.0).astype(BF16)
    pick_one = jnp.where(head_col == head_row * HEAD_DIM, 1.0, 0.0).astype(BF16)
    place = lax.broadcasted_iota(jnp.int32, (length, LANES), 0)

    def stack(tile):
        return jnp.concatenate([tile * lane_b[h] for h in range(4)], axis=0)

    def combine(tile):
        total = tile[:HEAD_DIM] * lane_f[0]
        for h in range(1, 4):
            total = total + tile[h * length : (h + 1) * length] * lane_f[h]
        return total

    def per_row(values):
        return values.reshape(rows, length, values.shape[-1])

    def unit(raw):
        parts = []
        for start in range(0, width, QUAD):
            piece = raw[:, start : start + QUAD]
            parts.append(nn((piece * piece).astype(BF16), blocks))
        return lax.rsqrt(jnp.concatenate(parts, axis=1) + 1e-06)

    def project_q(slot, normed_b):
        query_raw = nn(normed_b, wqkv[:, :width])
        q_inv = unit(query_raw)
        qa[:, pl.ds(slot * length, length), :] = per_row((query_raw * q_inv).astype(BF16))
        return query_raw, q_inv

    def project_kv(slot):
        block = (x_ref[...] if slot == 0 else xg[slot]).reshape(count, width)
        mask = jnp.concatenate(
            [jnp.where(place < cg[slot, r : r + 1, :], 1.0, 0.0) for r in range(rows)], axis=0
        )
        mask_wide = jnp.concatenate([mask] * (width // LANES), axis=1)
        normed, inverse = norm_stats(block.astype(F32))
        normed_b = normed.astype(BF16)
        if slot == 0:
            loads[0].wait()
        key_raw = nn(normed_b, wqkv[:, width : 2 * width])
        value = nn(normed_b, wqkv[:, 2 * width :])
        k_inv = unit(key_raw)
        at = pl.ds(slot * length, length)
        ka[:, at, :] = per_row((key_raw * k_inv * mask_wide).astype(BF16))
        va[:, at, :] = per_row((value * mask_wide).astype(BF16))
        ma[:, at, :] = per_row(mask.astype(BF16))
        return normed, inverse, normed_b, key_raw, k_inv, mask_wide

    normed, inverse, normed_b, key_raw, k_inv, mask_wide = project_kv(0)
    query_raw, q_inv = project_q(0, normed_b)
    c_across.wait_recv()
    c_onward.start()
    c_near.wait_recv()
    x_near.wait_recv()
    normed_near = project_kv(1)[2]
    x_across.wait_recv()
    x_onward.start()
    normed_across = project_kv(2)[2]
    c_onward.wait_recv()
    x_onward.wait_recv()
    normed_far = project_kv(3)[2]

    logit = 8.0 / HEAD_DIM

    @pl.loop(0, rows)
    def _(r):
        for qd in range(quads):
            cs = slice(qd * QUAD, (qd + 1) * QUAD)
            key, value = ka[r, :, cs], va[r, :, cs]
            score = jnp.exp(nt(stack(qa[r, 0:length, cs]), key) * logit - 8.0)
            score_b = score.astype(BF16)
            part = 1.0 / nn(score_b, ma[r])
            part = jnp.concatenate([part, part], axis=1)
            probs[r, qd] = score * part
            att_ref[r, :, cs] = combine(nn(score_b, value) * part)
            ivb_ref[r, :, cs] = combine(part)

    pending = {}

    def order(c):
        near = (x_pos, lo, x_peer, lo_peer) if c == 5 else (lo, x_pos, lo_peer, x_peer)
        return near

    def chunk(c):
        return bufs[9 * c : 9 * c + 9]

    def begin(c, left, right):
        part, from_core = chunk(c)[:2]
        n, r, c4 = part.shape[-3:]
        full = tn(left, right) * scale
        for l in range(SECTORS):
            piece = full[:, l * c4 : (l + 1) * c4].reshape(n, 2, r, c4).astype(BF16)
            for low in range(2):
                where = (l // 2, low) if c == 5 else (low, l // 2)
                part[(l % 2,) + where] = piece[:, low]
        at = 12 + 3 * c
        copy = remote(part.at[1 - core], from_core, sem_s.at[at], sem_r.at[at], core_peer)
        copy.start()
        pending[c] = copy

    def add(*terms):
        total = terms[0].astype(F32)
        for term in terms[1:]:
            total = total + term.astype(F32)
        return total.astype(BF16)

    def second(c):
        part, from_core, to_one, from_one = chunk(c)[:4]
        first_pos, _, first_peer, _ = order(c)
        pending[c].wait()
        to_one[...] = add(part[core, 1 - first_pos], from_core[1 - first_pos])
        at = 12 + 3 * c + 1
        copy = remote(to_one, from_one, sem_s.at[at], sem_r.at[at], first_peer)
        copy.start()
        pending[c] = copy

    def third(c):
        part, from_core, _, from_one, to_two, from_two = chunk(c)[:6]
        one, two, _, peer = order(c)
        pending[c].wait()
        to_two[...] = add(part[core, one, 1 - two], from_core[one, 1 - two], from_one[1 - two])
        at = 12 + 3 * c + 2
        copy = remote(to_two, from_two, sem_s.at[at], sem_r.at[at], peer)
        copy.start()
        pending[c] = copy

    def lat_copy(c, offset):
        total, from_lat = chunk(c)[6:8]
        target = hi_peer(offset)
        return remote(
            total.at[target], from_lat.at[offset - 1],
            lat_s.at[c, offset - 1], lat_r.at[c, offset - 1], (target * 2 + lo, lon),
        )

    def fourth(c):
        part, from_core, _, from_one, _, from_two, total, _, _ = chunk(c)
        one, two, _, _ = order(c)
        pending[c].wait()
        total[...] = add(part[core, one, two], from_core[one, two], from_one[two], from_two[...])

        @pl.loop(1, half_n)
        def _(offset):
            lat_copy(c, offset).start()

    def fifth(c):
        total, from_lat, everyone = chunk(c)[6:9]

        @pl.loop(1, half_n)
        def _(offset):
            lat_copy(c, offset).wait()

        everyone[lon] = (
            total[hi].astype(F32) + jnp.sum(from_lat[...].astype(F32), axis=0)
        ).astype(BF16)
        copies = []
        for i, peer in enumerate((x_peer, far_peer, core_peer)):
            copy = remote(
                everyone.at[lon], everyone.at[lon], all_s.at[c, i], all_r.at[c, i], peer
            )
            copy.start()
            copies.append(copy)
        pending[c] = copies

    stores = []

    def store(src, dst):
        copy = pltpu.make_async_copy(src, dst, out_sem.at[len(stores)])
        copy.start()
        stores.append(copy)

    def finish(c, out, first):
        everyone = chunk(c)[8]
        c4 = everyone.shape[-1]
        for copy in pending[c]:
            copy.wait()
        for l in range(SECTORS):
            out[:, first + l * c4 : first + (l + 1) * c4] = everyone[l].astype(F32)

    for load in loads[1:]:
        load.wait()
    tokens = x_ref[...].reshape(count, width).astype(F32)
    cotangent = cot_ref[...].reshape(count, width).astype(F32)
    grad_branch = (mask_wide * cotangent).astype(BF16)
    attended = att_ref[...].reshape(count, width)
    attended_b = attended.astype(BF16)
    middle = tokens + mask_wide * nn(attended_b, wout[...])
    normed_two, inverse_two = norm_stats(middle)
    normed_two_b = normed_two.astype(BF16)
    lifted = nn(normed_two_b, wup[...])
    root = math.sqrt(2.0 / math.pi)
    square = lifted * lifted
    curve = jnp.tanh(root * lifted * (1.0 + 0.044715 * square))
    half = 0.5 * (1.0 + curve)
    active = (lifted * half).astype(BF16)
    slope = half + 0.5 * lifted * (1.0 - curve * curve) * (root * (1.0 + 3 * 0.044715 * square))
    begin(0, active, grad_branch)

    grad_lifted = (slope * nt(grad_branch, wdown[...])).astype(BF16)
    grad_middle = cotangent + norm_back(nt(grad_lifted, wup[...]), normed_two, inverse_two)
    second(0)
    grad_attn = (mask_wide * grad_middle).astype(BF16)
    grad_attended = nt(grad_attn, wout[...]).astype(BF16)
    gaall[0] = per_row(grad_attended)
    g_near, g_across, g_onward = gather(gaall.at[0], gaall, 3)
    product = per_row(grad_attended.astype(F32) * attended)
    for r in range(rows):
        high, low = split_two(ivb_ref[r])
        part = nt(pick_one, high) + nt(pick_one, low)
        high, low = split_two(product[r])
        delta = nt(pick_sum, high) + nt(pick_sum, low)
        pair = jnp.concatenate([part, delta], axis=0)
        stats[0, r] = jnp.concatenate([pair, jnp.zeros_like(pair)], axis=1)
    s_near, s_across, s_onward = gather(stats.at[0], stats, 6)

    begin(1, normed_two_b, grad_lifted)
    begin(2, attended_b, grad_attn)
    third(0)
    second(1)
    bo_ref[...] = per_row((middle + mask_wide * nn(active, wdown[...])).astype(BF16))
    store(bo_ref, bo_hbm)
    project_q(1, normed_near)
    project_q(2, normed_across)
    project_q(3, normed_far)
    second(2)
    g_across.wait_recv()
    g_onward.start()
    s_across.wait_recv()
    s_onward.start()

    @pl.loop(0, rows)
    def _(r):
        for qd in range(quads):
            cs = slice(qd * QUAD, (qd + 1) * QUAD)
            key, value = ka[r, :, cs], va[r, :, cs]
            tall = stack(gaall[0, r, :, cs])
            delta = jnp.sum(
                tall.astype(F32) * jnp.concatenate([att_ref[r, :, cs]] * 4, axis=0),
                axis=-1,
                keepdims=True,
            )
            back = (probs[r, qd] * (nt(tall, value) - delta) * logit).astype(BF16)
            dq_ref[r, :, cs] = combine(nn(back, key))

    def head_back(grad, raw, inv):
        return inv * (grad - raw * (inv * inv) * head_mean(raw * grad, blocks))

    third(1)
    grad_q = head_back(dq_ref[...].reshape(count, width), query_raw, q_inv).astype(BF16)
    begin(3, normed_b, grad_q)
    fourth(0)
    third(2)
    second(3)
    for copy in (g_near, s_near, g_onward, s_onward):
        copy.wait_recv()

    @pl.loop(0, rows)
    def _(r):
        stat = jnp.concatenate([stats[s, r][:, :length] for s in range(SECTORS)], axis=1)
        for qd in range(quads):
            cs = slice(qd * QUAD, (qd + 1) * QUAD)
            query = qa[r, :, cs]
            grad = jnp.concatenate([gaall[s, r, :, cs] for s in range(SECTORS)], axis=0)

            def spread(base):
                return jnp.concatenate(
                    [
                        jnp.broadcast_to(stat[base + h : base + h + 1], (length, QUAD))
                        for h in range(qd * 4, qd * 4 + 4)
                    ],
                    axis=0,
                )

            score = jnp.exp(nt(stack(ka[r, 0:length, cs]), query) * logit - 8.0) * spread(0)
            deep = nt(stack(va[r, 0:length, cs]), grad)
            back = (score * (deep - spread(heads)) * logit).astype(BF16)
            dk_ref[r, :, cs] = combine(nn(back, query))
            dv_ref[r, :, cs] = combine(nn(score.astype(BF16), grad))

    grad_v = (dv_ref[...].reshape(count, width) * mask_wide).astype(BF16)
    begin(4, normed_b, grad_v)
    fourth(1)
    third(3)
    grad_k = head_back(
        dk_ref[...].reshape(count, width) * mask_wide, key_raw, k_inv
    ).astype(BF16)
    begin(5, normed_b, grad_k)
    second(4)
    fourth(2)
    fifth(0)
    second(5)
    grad_normed = (
        nt(grad_q, wqkv[:, :width])
        + nt(grad_k, wqkv[:, width : 2 * width])
        + nt(grad_v, wqkv[:, 2 * width :])
    )
    gt_ref[...] = per_row((grad_middle + norm_back(grad_normed, normed, inverse)).astype(BF16))
    store(gt_ref, gt_hbm)
    third(4)
    fourth(3)
    third(5)
    fifth(1)
    finish(0, gdown, 0)
    store(gdown, gdown_hbm)
    fourth(4)
    fifth(2)
    fourth(5)
    finish(1, gup, 0)
    store(gup, gup_hbm)
    fifth(3)
    fifth(4)
    finish(2, gout, 0)
    store(gout, gout_hbm)
    finish(3, gqkv, 0)
    for group in (
        (g_near, g_across, g_onward), (s_near, s_across, s_onward),
        (x_near, x_across, x_onward), (c_near, c_across, c_onward),
    ):
        for copy in group:
            copy.wait_send()
    fifth(5)
    finish(4, gqkv, 2 * width)
    finish(5, gqkv, width)
    store(gqkv, gqkv_hbm)
    for copy in stores:
        copy.wait()


def hand_over(*refs):
    sems = refs[12]
    copies = [pltpu.make_async_copy(refs[i], refs[6 + i], sems.at[i]) for i in range(6)]
    for copy in copies:
        copy.start()
    for copy in copies:
        copy.wait()


def local(lat_n, tokens, ocean_count, w_qkv, w_out, w_up, w_down, cotangent):
    rows, length, width = tokens.shape
    heads = width // HEAD_DIM
    hidden = w_up.shape[1]
    half_n = lat_n // 2
    scale = 1.0 / math.sqrt(rows * lat_n * length * SECTORS)
    quads = width // QUAD
    full = length * SECTORS
    out_shape = (
        jax.ShapeDtypeStruct(tokens.shape, BF16),
        jax.ShapeDtypeStruct(tokens.shape, BF16),
        jax.ShapeDtypeStruct((width // lat_n, 3 * width), F32),
        jax.ShapeDtypeStruct((width // lat_n, width), F32),
        jax.ShapeDtypeStruct((width // lat_n, hidden), F32),
        jax.ShapeDtypeStruct((hidden // lat_n, width), F32),
    )
    scratch = [pltpu.VMEM(a.shape, BF16) for a in (cotangent, w_qkv, w_out, w_up, w_down)]
    scratch += [pltpu.VMEM(a.shape, a.dtype) for a in out_shape]
    scratch += [
        pltpu.VMEM((SECTORS, rows, length, width), BF16),
        pltpu.VMEM((SECTORS, -(-rows // 8) * 8, LANES), jnp.int32),
        pltpu.VMEM((rows, full, width), BF16),
        pltpu.VMEM((rows, full, width), BF16),
        pltpu.VMEM((rows, full, LANES), BF16),
        pltpu.VMEM((rows, full, width), BF16),
        pltpu.VMEM((rows, quads, 4 * length, full), F32),
        pltpu.VMEM((rows, length, width), F32),
        pltpu.VMEM((rows, length, width), F32),
        pltpu.VMEM((rows, length, width), F32),
        pltpu.VMEM((rows, length, width), F32),
        pltpu.VMEM((rows, length, width), F32),
        pltpu.VMEM((SECTORS, rows, length, width), BF16),
        pltpu.VMEM((SECTORS, rows, 2 * heads, LANES), F32),
        pltpu.SemaphoreType.DMA((30,)),
        pltpu.SemaphoreType.DMA((30,)),
        pltpu.SemaphoreType.DMA((6, half_n - 1)),
        pltpu.SemaphoreType.DMA((6, half_n - 1)),
        pltpu.SemaphoreType.DMA((6, 3)),
        pltpu.SemaphoreType.DMA((6, 3)),
        pltpu.SemaphoreType.DMA((5,)),
        pltpu.SemaphoreType.DMA((6,)),
    ]
    for tall, broad in ((hidden, width), (width, hidden)) + ((width, width),) * 4:
        r, c4 = tall // lat_n, broad // SECTORS
        scratch += [
            pltpu.VMEM((2, 2, 2, half_n, r, c4), BF16),
            pltpu.VMEM((2, 2, half_n, r, c4), BF16),
            pltpu.VMEM((2, half_n, r, c4), BF16),
            pltpu.VMEM((2, half_n, r, c4), BF16),
            pltpu.VMEM((half_n, r, c4), BF16),
            pltpu.VMEM((half_n, r, c4), BF16),
            pltpu.VMEM((half_n, r, c4), BF16),
            pltpu.VMEM((half_n - 1, r, c4), BF16),
            pltpu.VMEM((SECTORS, r, c4), BF16),
        ]
    vmem = pl.BlockSpec(memory_space=pltpu.VMEM)
    hbm = pl.BlockSpec(memory_space=pl.ANY)
    results = pl.pallas_call(
        functools.partial(kernel, lat_n, scale),
        out_shape=out_shape,
        in_specs=[vmem] * 2 + [hbm] * 5,
        out_specs=(hbm,) * 6,
        scratch_shapes=scratch,
        compiler_params=pltpu.CompilerParams(
            collective_id=0, has_side_effects=True, vmem_limit_bytes=56 * 1024 * 1024
        ),
    )(tokens, ocean_count, cotangent, w_qkv, w_out, w_up, w_down)
    return pl.pallas_call(
        hand_over,
        out_shape=out_shape,
        in_specs=[pl.BlockSpec(memory_space=pltpu.HBM)] * 6,
        out_specs=(hbm,) * 6,
        scratch_shapes=[pltpu.SemaphoreType.DMA((6,))],
    )(*results)


def solution(mesh):
    rows = P("lat", "lon", None)
    in_specs = (rows, P("lat", "lon"), P(), P(), P(), P(), rows)
    out_specs = (rows, rows, P("lat", None), P("lat", None), P("lat", None), P("lat", None))
    return jax.shard_map(
        functools.partial(local, mesh.shape["lat"]),
        mesh=mesh,
        in_specs=in_specs,
        out_specs=out_specs,
        check_vma=False,
    )
```

time: 75.8 us -> 108 us (1.42)
  Pallas kernels: 65.4 us -> 106 us
  local copies, waits for them, and re-layouts: 7.14 us -> 1.31 us
  other arithmetic: 2.38 us -> 0 us
    pallas_call x1 -> x2, Pallas kernels: 65.4 us -> 106 us  [the longest x1 61.1 us: local(): pl.pallas_call(functools.partial(kernel, lat_n, scale), out_shape=out_sha...]
    unnamed x12 -> x1, local copies, waits for them, and re-layouts: 7.14 us -> 1.31 us
    concatenate x1 -> x0, other arithmetic: 1.65 us -> none  [local(): extended = jnp.concatenate([tokens, mask], axis=-1)]
where the time goes in v2:
time: 108 us
  Pallas kernels  106 us (98%)
  local copies, waits for them, and re-layouts  1.31 us (1%)
    pallas_call x1, Pallas kernels, local(): pl.pallas_call(functools.partial(kernel, lat_n, scale), out_shape=out_sha...  61.1 us
    pallas_call x1, Pallas kernels, local(): pl.pallas_call(hand_over, out_shape=out_shape, in_specs=[pl.BlockSpec(mem...  44.8 us

profile of v2, /device:TPU:0, one launch (start us, length us, event | category | flops | bytes accessed | tf_op | source)
XLA Modules:
  0.0 107.9 jit_solution(15453209944290653251)
XLA Ops:
  0.6 1.3 %copy.13.refs_1_ = s32[3,1]{1,0:T(4,128)} copy(s32[3,1]{0,1:T(1,128)} %param.8) | data formatting | bytes 24 | tf_op args[1]
  1.9 61.1 %shard_map.118 = (bf16[3,64,512]{2,1,0:T(8,128)(2,1)}, bf16[3,64,512]{2,1,0:T(8,128)(2,1)}, f32[64,1536]{1,0:T(8,128)}, f32[64,512]{1,0:T(8,128)}, f32[64,1024]{1,0:T(8,128)}, /*index=5*/f32[128,512]{1,0:T(8,128)}) custom-call(bf16[3,64,512]{2,1,0:T(8,128)(2,1)} %refs_0_.1, s32[3,1]{1,0:T(4,128)} %copy.13.refs_1_, bf16[3,64,512]{2,1,0:T(8,128)(2,1)} %refs_2_.1, ...), custom_call_target="tpu_custom_call" | custom-call | tf_op jit(solution)/shard_map/pallas_call | solution.py:528
  63.1 44.8 %shard_map.119 = (bf16[3,64,512]{2,1,0:T(8,128)(2,1)}, bf16[3,64,512]{2,1,0:T(8,128)(2,1)}, f32[64,1536]{1,0:T(8,128)}, f32[64,512]{1,0:T(8,128)}, f32[64,1024]{1,0:T(8,128)}, /*index=5*/f32[128,512]{1,0:T(8,128)}) custom-call(bf16[3,64,512]{2,1,0:T(8,128)(2,1)} %get-tuple-element.12.refs_0_, bf16[3,64,512]{2,1,0:T(8,128)(2,1)} %get-tuple-element.13.refs_1_, ...), custom_call_target="tpu_custom_call" | custom-call | tf_op jit(solution)/shard_map/pallas_call | solution.py:538

commit v3 on v2

--- a/solution.py
+++ b/solution.py
@@ -100,7 +100,9 @@
         loads.append(load)
 
     cg[0] = jnp.zeros_like(cg[0])
-    cg[0, 0:rows] = jnp.broadcast_to(count_ref[...], (rows, LANES))
+    counts = count_ref[...]
+    for r in range(rows):
+        cg[0, r : r + 1] = jnp.broadcast_to(counts[:, r : r + 1], (1, LANES))
     pl.semaphore_wait(barrier, 4 + half_n - 1)
 
     def remote(src, dst, send, recv, peer):
@@ -196,8 +198,7 @@
 
     logit = 8.0 / HEAD_DIM
 
-    @pl.loop(0, rows)
-    def _(r):
+    for r in range(rows):
         for qd in range(quads):
             cs = slice(qd * QUAD, (qd + 1) * QUAD)
             key, value = ka[r, :, cs], va[r, :, cs]
@@ -348,21 +349,20 @@
 
     begin(1, normed_two_b, grad_lifted)
     begin(2, attended_b, grad_attn)
-    third(0)
     second(1)
+    second(2)
     bo_ref[...] = per_row((middle + mask_wide * nn(active, wdown[...])).astype(BF16))
     store(bo_ref, bo_hbm)
     project_q(1, normed_near)
     project_q(2, normed_across)
     project_q(3, normed_far)
-    second(2)
+    third(0)
     g_across.wait_recv()
     g_onward.start()
     s_across.wait_recv()
     s_onward.start()
 
-    @pl.loop(0, rows)
-    def _(r):
+    for r in range(rows):
         for qd in range(quads):
             cs = slice(qd * QUAD, (qd + 1) * QUAD)
             key, value = ka[r, :, cs], va[r, :, cs]
@@ -378,17 +378,14 @@
     def head_back(grad, raw, inv):
         return inv * (grad - raw * (inv * inv) * head_mean(raw * grad, blocks))
 
-    third(1)
     grad_q = head_back(dq_ref[...].reshape(count, width), query_raw, q_inv).astype(BF16)
     begin(3, normed_b, grad_q)
-    fourth(0)
-    third(2)
-    second(3)
     for copy in (g_near, s_near, g_onward, s_onward):
         copy.wait_recv()
-
-    @pl.loop(0, rows)
-    def _(r):
+    second(3)
+    third(1)
+
+    for r in range(rows):
         stat = jnp.concatenate([stats[s, r][:, :length] for s in range(SECTORS)], axis=1)
         for qd in range(quads):
             cs = slice(qd * QUAD, (qd + 1) * QUAD)
@@ -412,16 +409,18 @@
 
     grad_v = (dv_ref[...].reshape(count, width) * mask_wide).astype(BF16)
     begin(4, normed_b, grad_v)
-    fourth(1)
-    third(3)
+    third(2)
+    fourth(0)
     grad_k = head_back(
         dk_ref[...].reshape(count, width) * mask_wide, key_raw, k_inv
     ).astype(BF16)
     begin(5, normed_b, grad_k)
     second(4)
+    second(5)
+    third(3)
+    fourth(1)
     fourth(2)
     fifth(0)
-    second(5)
     grad_normed = (
         nt(grad_q, wqkv[:, :width])
         + nt(grad_k, wqkv[:, width : 2 * width])
@@ -534,11 +533,11 @@
         compiler_params=pltpu.CompilerParams(
             collective_id=0, has_side_effects=True, vmem_limit_bytes=56 * 1024 * 1024
         ),
-    )(tokens, ocean_count, cotangent, w_qkv, w_out, w_up, w_down)
+    )(tokens, ocean_count.T, cotangent, w_qkv, w_out, w_up, w_down)
     return pl.pallas_call(
         hand_over,
         out_shape=out_shape,
-        in_specs=[pl.BlockSpec(memory_space=pltpu.HBM)] * 6,
+        in_specs=[vmem] * 6,
         out_specs=(hbm,) * 6,
         scratch_shapes=[pltpu.SemaphoreType.DMA((6,))],
     )(*results)

time: 108 us -> 58.6 us (0.54)
  Pallas kernels: 106 us -> 57.8 us
  local copies, waits for them, and re-layouts: 1.31 us -> 0 us
    pallas_call x1, Pallas kernels: 44.8 us -> 2.56 us  [local(): pl.pallas_call(hand_over, out_shape=out_shape, in_specs=[vmem] * 6, out_s...]
    pallas_call x1, Pallas kernels: 61.1 us -> 55.2 us  [local(): pl.pallas_call(functools.partial(kernel, lat_n, scale), out_shape=out_sha...]
    unnamed x1 -> x0, local copies, waits for them, and re-layouts: 1.31 us -> none
where the time goes in v3:
time: 58.6 us; the launch traced here: 58.4 us
  Pallas kernels  57.8 us (99%)
  between operations  0.64 us (1%)
    pallas_call x1, Pallas kernels, local(): pl.pallas_call(functools.partial(kernel, lat_n, scale), out_shape=out_sha...  55.2 us
    pallas_call x1, Pallas kernels, local(): pl.pallas_call(hand_over, out_shape=out_shape, in_specs=[vmem] * 6, out_s...  2.56 us

profile of v3, /device:TPU:0, one launch (start us, length us, event | category | flops | bytes accessed | tf_op | source)
XLA Modules:
  0.0 58.4 jit_solution(3130913085825342165)
XLA Ops:
  0.6 55.2 %shard_map.118 = (bf16[3,64,512]{2,1,0:T(8,128)(2,1)}, bf16[3,64,512]{2,1,0:T(8,128)(2,1)}, f32[64,1536]{1,0:T(8,128)}, f32[64,512]{1,0:T(8,128)}, f32[64,1024]{1,0:T(8,128)}, /*index=5*/f32[128,512]{1,0:T(8,128)}) custom-call(bf16[3,64,512]{2,1,0:T(8,128)(2,1)} %refs_0_.1, s32[1,3]{1,0:T(1,128)} %bitcast.1, bf16[3,64,512]{2,1,0:T(8,128)(2,1)} %refs_2_.1, ...), custom_call_target="tpu_custom_call" | custom-call | tf_op jit(solution)/shard_map/pallas_call | solution.py:527
  55.8 2.6 %shard_map.119 = (bf16[3,64,512]{2,1,0:T(8,128)(2,1)}, bf16[3,64,512]{2,1,0:T(8,128)(2,1)}, f32[64,1536]{1,0:T(8,128)}, f32[64,512]{1,0:T(8,128)}, f32[64,1024]{1,0:T(8,128)}, /*index=5*/f32[128,512]{1,0:T(8,128)}) custom-call(bf16[3,64,512]{2,1,0:T(8,128)(2,1)} %get-tuple-element.12.refs_0_, bf16[3,64,512]{2,1,0:T(8,128)(2,1)} %get-tuple-element.13.refs_1_, ...), custom_call_target="tpu_custom_call" | custom-call | tf_op jit(solution)/shard_map/pallas_call | solution.py:537

commit v4 on v3

--- a/solution.py
+++ b/solution.py
@@ -103,6 +103,8 @@
     counts = count_ref[...]
     for r in range(rows):
         cg[0, r : r + 1] = jnp.broadcast_to(counts[:, r : r + 1], (1, LANES))
+    normed, inverse = norm_stats(x_ref[...].reshape(count, width).astype(F32))
+    normed_b = normed.astype(BF16)
     pl.semaphore_wait(barrier, 4 + half_n - 1)
 
     def remote(src, dst, send, recv, peer):
@@ -120,7 +122,19 @@
         return near, across, onward
 
     c_near, c_across, c_onward = gather(cg.at[0], cg, 9)
-    x_near, x_across, x_onward = gather(x_ref, xg, 0)
+    x_near = remote(x_ref, xg.at[1], sem_s.at[0], sem_r.at[0], core_peer)
+    x_across, x_onward = [], []
+    for r in range(rows):
+        at = 30 + 2 * r
+        x_across.append(
+            remote(x_ref.at[r], xg.at[2, r], sem_s.at[at], sem_r.at[at], x_peer)
+        )
+        x_onward.append(
+            remote(xg.at[2, r], xg.at[3, r], sem_s.at[at + 1], sem_r.at[at + 1], core_peer)
+        )
+        x_across[r].start()
+        if r == 0:
+            x_near.start()
 
     lane = lax.broadcasted_iota(jnp.int32, (1, QUAD), 1) // HEAD_DIM
     lane_f = [jnp.where(lane == h, 1.0, 0.0).astype(F32) for h in range(4)]
@@ -157,48 +171,58 @@
             parts.append(nn((piece * piece).astype(BF16), blocks))
         return lax.rsqrt(jnp.concatenate(parts, axis=1) + 1e-06)
 
-    def project_q(slot, normed_b):
+    def query_of(normed_b):
         query_raw = nn(normed_b, wqkv[:, :width])
         q_inv = unit(query_raw)
-        qa[:, pl.ds(slot * length, length), :] = per_row((query_raw * q_inv).astype(BF16))
-        return query_raw, q_inv
-
-    def project_kv(slot):
-        block = (x_ref[...] if slot == 0 else xg[slot]).reshape(count, width)
-        mask = jnp.concatenate(
-            [jnp.where(place < cg[slot, r : r + 1, :], 1.0, 0.0) for r in range(rows)], axis=0
-        )
+        return (query_raw * q_inv).astype(BF16), query_raw, q_inv
+
+    def mask_of(slot, r):
+        return jnp.where(place < cg[slot, r : r + 1, :], 1.0, 0.0)
+
+    def kv_of(normed_b, mask):
         mask_wide = jnp.concatenate([mask] * (width // LANES), axis=1)
-        normed, inverse = norm_stats(block.astype(F32))
-        normed_b = normed.astype(BF16)
-        if slot == 0:
-            loads[0].wait()
         key_raw = nn(normed_b, wqkv[:, width : 2 * width])
         value = nn(normed_b, wqkv[:, 2 * width :])
         k_inv = unit(key_raw)
-        at = pl.ds(slot * length, length)
-        ka[:, at, :] = per_row((key_raw * k_inv * mask_wide).astype(BF16))
-        va[:, at, :] = per_row((value * mask_wide).astype(BF16))
-        ma[:, at, :] = per_row(mask.astype(BF16))
-        return normed, inverse, normed_b, key_raw, k_inv, mask_wide
-
-    normed, inverse, normed_b, key_raw, k_inv, mask_wide = project_kv(0)
-    query_raw, q_inv = project_q(0, normed_b)
+        key = (key_raw * k_inv * mask_wide).astype(BF16)
+        return key, (value * mask_wide).astype(BF16), key_raw, k_inv, mask_wide
+
+    mask = jnp.concatenate([mask_of(0, r) for r in range(rows)], axis=0)
+    loads[0].wait()
+    key, value, key_raw, k_inv, mask_wide = kv_of(normed_b, mask)
+    ka[:, 0:length, :], va[:, 0:length, :] = per_row(key), per_row(value)
+    ma[:, 0:length, :] = per_row(mask.astype(BF16))
+    query, query_raw, q_inv = query_of(normed_b)
+    qa[:, 0:length, :] = per_row(query)
+    normed_t = normed_b.T
+
     c_across.wait_recv()
     c_onward.start()
     c_near.wait_recv()
     x_near.wait_recv()
-    normed_near = project_kv(1)[2]
-    x_across.wait_recv()
-    x_onward.start()
-    normed_across = project_kv(2)[2]
+    normed_near = norm_stats(xg[1].reshape(count, width).astype(F32))[0].astype(BF16)
+    mask = jnp.concatenate([mask_of(1, r) for r in range(rows)], axis=0)
+    key, value = kv_of(normed_near, mask)[:2]
+    at = slice(length, 2 * length)
+    ka[:, at, :], va[:, at, :] = per_row(key), per_row(value)
+    ma[:, at, :] = per_row(mask.astype(BF16))
+
+    logit = 8.0 / HEAD_DIM
+    normed_far = []
+    x_across[0].wait_recv()
+    x_onward[0].start()
     c_onward.wait_recv()
-    x_onward.wait_recv()
-    normed_far = project_kv(3)[2]
-
-    logit = 8.0 / HEAD_DIM
-
     for r in range(rows):
+        x_onward[r].wait_recv()
+        if r + 1 < rows:
+            x_across[r + 1].wait_recv()
+            x_onward[r + 1].start()
+        block = jnp.concatenate([xg[2, r], xg[3, r]], axis=0).astype(F32)
+        normed_far.append(norm_stats(block)[0].astype(BF16))
+        mask = jnp.concatenate([mask_of(2, r), mask_of(3, r)], axis=0)
+        far_key, far_value = kv_of(normed_far[r], mask)[:2]
+        at = slice(2 * length, 4 * length)
+        ka[r, at, :], va[r, at, :], ma[r, at, :] = far_key, far_value, mask.astype(BF16)
         for qd in range(quads):
             cs = slice(qd * QUAD, (qd + 1) * QUAD)
             key, value = ka[r, :, cs], va[r, :, cs]
@@ -222,7 +246,7 @@
     def begin(c, left, right):
         part, from_core = chunk(c)[:2]
         n, r, c4 = part.shape[-3:]
-        full = tn(left, right) * scale
+        full = nn(normed_t, right) if left is None else tn(left, right)
         for l in range(SECTORS):
             piece = full[:, l * c4 : (l + 1) * c4].reshape(n, 2, r, c4).astype(BF16)
             for low in range(2):
@@ -309,7 +333,7 @@
         for copy in pending[c]:
             copy.wait()
         for l in range(SECTORS):
-            out[:, first + l * c4 : first + (l + 1) * c4] = everyone[l].astype(F32)
+            out[:, first + l * c4 : first + (l + 1) * c4] = everyone[l].astype(F32) * scale
 
     for load in loads[1:]:
         load.wait()
@@ -351,11 +375,10 @@
     begin(2, attended_b, grad_attn)
     second(1)
     second(2)
-    bo_ref[...] = per_row((middle + mask_wide * nn(active, wdown[...])).astype(BF16))
-    store(bo_ref, bo_hbm)
-    project_q(1, normed_near)
-    project_q(2, normed_across)
-    project_q(3, normed_far)
+    qa[:, length : 2 * length, :] = per_row(query_of(normed_near)[0])
+    qa[:, 2 * length : 4 * length, :] = query_of(
+        jnp.concatenate(normed_far, axis=0)
+    )[0].reshape(rows, 2 * length, width)
     third(0)
     g_across.wait_recv()
     g_onward.start()
@@ -379,7 +402,7 @@
         return inv * (grad - raw * (inv * inv) * head_mean(raw * grad, blocks))
 
     grad_q = head_back(dq_ref[...].reshape(count, width), query_raw, q_inv).astype(BF16)
-    begin(3, normed_b, grad_q)
+    begin(3, None, grad_q)
     for copy in (g_near, s_near, g_onward, s_onward):
         copy.wait_recv()
     second(3)
@@ -408,18 +431,18 @@
             dv_ref[r, :, cs] = combine(nn(score.astype(BF16), grad))
 
     grad_v = (dv_ref[...].reshape(count, width) * mask_wide).astype(BF16)
-    begin(4, normed_b, grad_v)
+    begin(4, None, grad_v)
     third(2)
     fourth(0)
     grad_k = head_back(
         dk_ref[...].reshape(count, width) * mask_wide, key_raw, k_inv
     ).astype(BF16)
-    begin(5, normed_b, grad_k)
+    begin(5, None, grad_k)
     second(4)
-    second(5)
     third(3)
     fourth(1)
     fourth(2)
+    second(5)
     fifth(0)
     grad_normed = (
         nt(grad_q, wqkv[:, :width])
@@ -430,6 +453,8 @@
     store(gt_ref, gt_hbm)
     third(4)
     fourth(3)
+    bo_ref[...] = per_row((middle + mask_wide * nn(active, wdown[...])).astype(BF16))
+    store(bo_ref, bo_hbm)
     third(5)
     fifth(1)
     finish(0, gdown, 0)
@@ -446,7 +471,7 @@
     finish(3, gqkv, 0)
     for group in (
         (g_near, g_across, g_onward), (s_near, s_across, s_onward),
-        (x_near, x_across, x_onward), (c_near, c_across, c_onward),
+        [x_near] + x_across + x_onward, (c_near, c_across, c_onward),
     ):
         for copy in group:
             copy.wait_send()
@@ -500,8 +525,8 @@
         pltpu.VMEM((rows, length, width), F32),
         pltpu.VMEM((SECTORS, rows, length, width), BF16),
         pltpu.VMEM((SECTORS, rows, 2 * heads, LANES), F32),
-        pltpu.SemaphoreType.DMA((30,)),
-        pltpu.SemaphoreType.DMA((30,)),
+        pltpu.SemaphoreType.DMA((30 + 2 * rows,)),
+        pltpu.SemaphoreType.DMA((30 + 2 * rows,)),
         pltpu.SemaphoreType.DMA((6, half_n - 1)),
         pltpu.SemaphoreType.DMA((6, half_n - 1)),
         pltpu.SemaphoreType.DMA((6, 3)),

time: 58.6 us -> 58.4 us (level)
  no operation moved by 1% of the time
where the time goes in v4:
time: 58.4 us; the launch traced here: 58.3 us
  Pallas kernels  57.6 us (99%)
  between operations  0.64 us (1%)
    pallas_call x1, Pallas kernels, local(): pl.pallas_call(functools.partial(kernel, lat_n, scale), out_shape=out_sha...  55.1 us
    pallas_call x1, Pallas kernels, local(): pl.pallas_call(hand_over, out_shape=out_shape, in_specs=[vmem] * 6, out_s...  2.56 us

profile of v4, /device:TPU:0, one launch (start us, length us, event | category | flops | bytes accessed | tf_op | source)
XLA Modules:
  0.0 58.3 jit_solution(4450169444697096048)
XLA Ops:
  0.6 55.1 %shard_map.118 = (bf16[3,64,512]{2,1,0:T(8,128)(2,1)}, bf16[3,64,512]{2,1,0:T(8,128)(2,1)}, f32[64,1536]{1,0:T(8,128)}, f32[64,512]{1,0:T(8,128)}, f32[64,1024]{1,0:T(8,128)}, /*index=5*/f32[128,512]{1,0:T(8,128)}) custom-call(bf16[3,64,512]{2,1,0:T(8,128)(2,1)} %refs_0_.1, s32[1,3]{1,0:T(1,128)} %bitcast.1, bf16[3,64,512]{2,1,0:T(8,128)(2,1)} %refs_2_.1, ...), custom_call_target="tpu_custom_call" | custom-call | tf_op jit(solution)/shard_map/pallas_call | solution.py:552
  55.7 2.6 %shard_map.119 = (bf16[3,64,512]{2,1,0:T(8,128)(2,1)}, bf16[3,64,512]{2,1,0:T(8,128)(2,1)}, f32[64,1536]{1,0:T(8,128)}, f32[64,512]{1,0:T(8,128)}, f32[64,1024]{1,0:T(8,128)}, /*index=5*/f32[128,512]{1,0:T(8,128)}) custom-call(bf16[3,64,512]{2,1,0:T(8,128)(2,1)} %get-tuple-element.12.refs_0_, bf16[3,64,512]{2,1,0:T(8,128)(2,1)} %get-tuple-element.13.refs_1_, ...), custom_call_target="tpu_custom_call" | custom-call | tf_op jit(solution)/shard_map/pallas_call | solution.py:562

commit v5 on v4

--- a/solution.py
+++ b/solution.py
@@ -61,9 +61,9 @@
     bo_hbm, gt_hbm, gqkv_hbm, gout_hbm, gup_hbm, gdown_hbm = refs[7:13]
     cot_ref, wqkv, wout, wup, wdown = refs[13:18]
     bo_ref, gt_ref, gqkv, gout, gup, gdown = refs[18:24]
-    xg, cg, ka, va, ma, qa, probs, att_ref, ivb_ref, dq_ref, dk_ref, dv_ref, gaall, stats = refs[24:38]
-    sem_s, sem_r, lat_s, lat_r, all_s, all_r, in_sem, out_sem = refs[38:46]
-    bufs = refs[46:]
+    xg, cg, ka, va, ma, qa, probs, att_ref, ivb_ref, dq_ref, dk_ref, dv_ref, gaall, stats, ntr = refs[24:39]
+    sem_s, sem_r, lat_s, lat_r, all_s, all_r, in_sem, out_sem = refs[39:47]
+    bufs = refs[47:]
     rows, length, width = x_ref.shape
     count = rows * length
     quads = width // QUAD
@@ -194,7 +194,7 @@
     ma[:, 0:length, :] = per_row(mask.astype(BF16))
     query, query_raw, q_inv = query_of(normed_b)
     qa[:, 0:length, :] = per_row(query)
-    normed_t = normed_b.T
+    ntr[0] = normed_b.T
 
     c_across.wait_recv()
     c_onward.start()
@@ -237,8 +237,7 @@
     pending = {}
 
     def order(c):
-        near = (x_pos, lo, x_peer, lo_peer) if c == 5 else (lo, x_pos, lo_peer, x_peer)
-        return near
+        return lo, x_pos, lo_peer, x_peer
 
     def chunk(c):
         return bufs[9 * c : 9 * c + 9]
@@ -246,12 +245,11 @@
     def begin(c, left, right):
         part, from_core = chunk(c)[:2]
         n, r, c4 = part.shape[-3:]
-        full = nn(normed_t, right) if left is None else tn(left, right)
+        full = tn(left, right)
         for l in range(SECTORS):
             piece = full[:, l * c4 : (l + 1) * c4].reshape(n, 2, r, c4).astype(BF16)
             for low in range(2):
-                where = (l // 2, low) if c == 5 else (low, l // 2)
-                part[(l % 2,) + where] = piece[:, low]
+                part[l % 2, low, l // 2] = piece[:, low]
         at = 12 + 3 * c
         copy = remote(part.at[1 - core], from_core, sem_s.at[at], sem_r.at[at], core_peer)
         copy.start()
@@ -291,11 +289,47 @@
             lat_s.at[c, offset - 1], lat_r.at[c, offset - 1], (target * 2 + lo, lon),
         )
 
+    def lon_send(c, grad):
+        send, received = chunk(c)[:2]
+        c4 = send.shape[-1]
+        for l in range(SECTORS):
+            send[l] = grad[:, l * c4 : (l + 1) * c4]
+        copies = []
+        for slot, peer in ((3, far_peer), (2, x_peer), (1, core_peer)):
+            at = 12 + 3 * c + slot - 1
+            copy = remote(
+                send.at[peer[1]], received.at[slot - 1], sem_s.at[at], sem_r.at[at], peer
+            )
+            copy.start()
+            copies.append(copy)
+        pending[c] = copies
+
+    def lon_sum(c):
+        send, received, part, from_one = chunk(c)[:4]
+        _, n, r, c4 = part.shape
+        for copy in pending[c]:
+            copy.wait()
+        full = nn(ntr[0], send[lon])
+        for slot in range(1, SECTORS):
+            full = full + nn(ntr[slot], received[slot - 1])
+        piece = full.reshape(n, 2, r, c4).astype(BF16)
+        for low in range(2):
+            part[low] = piece[:, low]
+        at = 30 + 2 * rows + c - 3
+        copy = remote(part.at[1 - lo], from_one, sem_s.at[at], sem_r.at[at], lo_peer)
+        copy.start()
+        pending[c] = copy
+
     def fourth(c):
         part, from_core, _, from_one, _, from_two, total, _, _ = chunk(c)
         one, two, _, _ = order(c)
         pending[c].wait()
-        total[...] = add(part[core, one, two], from_core[one, two], from_one[two], from_two[...])
+        if c >= 3:
+            total[...] = add(chunk(c)[2][lo], from_one[...])
+        else:
+            total[...] = add(
+                part[core, one, two], from_core[one, two], from_one[two], from_two[...]
+            )
 
         @pl.loop(1, half_n)
         def _(offset):
@@ -379,6 +413,9 @@
     qa[:, 2 * length : 4 * length, :] = query_of(
         jnp.concatenate(normed_far, axis=0)
     )[0].reshape(rows, 2 * length, width)
+    ntr[1] = normed_near.T
+    ntr[2] = jnp.concatenate([piece[:length] for piece in normed_far], axis=0).T
+    ntr[3] = jnp.concatenate([piece[length:] for piece in normed_far], axis=0).T
     third(0)
     g_across.wait_recv()
     g_onward.start()
@@ -402,10 +439,9 @@
         return inv * (grad - raw * (inv * inv) * head_mean(raw * grad, blocks))
 
     grad_q = head_back(dq_ref[...].reshape(count, width), query_raw, q_inv).astype(BF16)
-    begin(3, None, grad_q)
+    lon_send(3, grad_q)
     for copy in (g_near, s_near, g_onward, s_onward):
         copy.wait_recv()
-    second(3)
     third(1)
 
     for r in range(rows):
@@ -431,19 +467,18 @@
             dv_ref[r, :, cs] = combine(nn(score.astype(BF16), grad))
 
     grad_v = (dv_ref[...].reshape(count, width) * mask_wide).astype(BF16)
-    begin(4, None, grad_v)
+    lon_send(4, grad_v)
     third(2)
     fourth(0)
     grad_k = head_back(
         dk_ref[...].reshape(count, width) * mask_wide, key_raw, k_inv
     ).astype(BF16)
-    begin(5, None, grad_k)
-    second(4)
-    third(3)
+    lon_send(5, grad_k)
+    lon_sum(3)
     fourth(1)
     fourth(2)
-    second(5)
     fifth(0)
+    lon_sum(4)
     grad_normed = (
         nt(grad_q, wqkv[:, :width])
         + nt(grad_k, wqkv[:, width : 2 * width])
@@ -451,20 +486,19 @@
     )
     gt_ref[...] = per_row((grad_middle + norm_back(grad_normed, normed, inverse)).astype(BF16))
     store(gt_ref, gt_hbm)
-    third(4)
+    lon_sum(5)
     fourth(3)
     bo_ref[...] = per_row((middle + mask_wide * nn(active, wdown[...])).astype(BF16))
     store(bo_ref, bo_hbm)
-    third(5)
+    fourth(4)
     fifth(1)
+    fourth(5)
     finish(0, gdown, 0)
     store(gdown, gdown_hbm)
-    fourth(4)
     fifth(2)
-    fourth(5)
+    fifth(3)
     finish(1, gup, 0)
     store(gup, gup_hbm)
-    fifth(3)
     fifth(4)
     finish(2, gout, 0)
     store(gout, gout_hbm)
@@ -525,8 +559,9 @@
         pltpu.VMEM((rows, length, width), F32),
         pltpu.VMEM((SECTORS, rows, length, width), BF16),
         pltpu.VMEM((SECTORS, rows, 2 * heads, LANES), F32),
-        pltpu.SemaphoreType.DMA((30 + 2 * rows,)),
-        pltpu.SemaphoreType.DMA((30 + 2 * rows,)),
+        pltpu.VMEM((SECTORS, width, rows * length), BF16),
+        pltpu.SemaphoreType.DMA((33 + 2 * rows,)),
+        pltpu.SemaphoreType.DMA((33 + 2 * rows,)),
         pltpu.SemaphoreType.DMA((6, half_n - 1)),
         pltpu.SemaphoreType.DMA((6, half_n - 1)),
         pltpu.SemaphoreType.DMA((6, 3)),
@@ -534,15 +569,29 @@
         pltpu.SemaphoreType.DMA((5,)),
         pltpu.SemaphoreType.DMA((6,)),
     ]
-    for tall, broad in ((hidden, width), (width, hidden)) + ((width, width),) * 4:
+    for c, (tall, broad) in enumerate(
+        ((hidden, width), (width, hidden)) + ((width, width),) * 4
+    ):
         r, c4 = tall // lat_n, broad // SECTORS
+        if c < 3:
+            scratch += [
+                pltpu.VMEM((2, 2, 2, half_n, r, c4), BF16),
+                pltpu.VMEM((2, 2, half_n, r, c4), BF16),
+                pltpu.VMEM((2, half_n, r, c4), BF16),
+                pltpu.VMEM((2, half_n, r, c4), BF16),
+                pltpu.VMEM((half_n, r, c4), BF16),
+                pltpu.VMEM((half_n, r, c4), BF16),
+            ]
+        else:
+            scratch += [
+                pltpu.VMEM((SECTORS, rows * length, c4), BF16),
+                pltpu.VMEM((SECTORS - 1, rows * length, c4), BF16),
+                pltpu.VMEM((2, half_n, r, c4), BF16),
+                pltpu.VMEM((half_n, r, c4), BF16),
+                pltpu.VMEM((8, LANES), BF16),
+                pltpu.VMEM((8, LANES), BF16),
+            ]
         scratch += [
-            pltpu.VMEM((2, 2, 2, half_n, r, c4), BF16),
-            pltpu.VMEM((2, 2, half_n, r, c4), BF16),
-            pltpu.VMEM((2, half_n, r, c4), BF16),
-            pltpu.VMEM((2, half_n, r, c4), BF16),
-            pltpu.VMEM((half_n, r, c4), BF16),
-            pltpu.VMEM((half_n, r, c4), BF16),
             pltpu.VMEM((half_n, r, c4), BF16),
             pltpu.VMEM((half_n - 1, r, c4), BF16),
             pltpu.VMEM((SECTORS, r, c4), BF16),

time: 58.4 us -> 57.2 us (0.979)
  Pallas kernels: 57.6 us -> 56.4 us
    pallas_call x1, Pallas kernels: 55.1 us -> 53.9 us  [local(): pl.pallas_call(functools.partial(kernel, lat_n, scale), out_shape=out_sha...]
where the time goes in v5:
time: 57.2 us; the launch traced here: 57.1 us
  Pallas kernels  56.4 us (99%)
  between operations  0.64 us (1%)
    pallas_call x1, Pallas kernels, local(): pl.pallas_call(functools.partial(kernel, lat_n, scale), out_shape=out_sha...  53.9 us
    pallas_call x1, Pallas kernels, local(): pl.pallas_call(hand_over, out_shape=out_shape, in_specs=[vmem] * 6, out_s...  2.56 us

profile of v5, /device:TPU:0, one launch (start us, length us, event | category | flops | bytes accessed | tf_op | source)
XLA Modules:
  0.0 57.1 jit_solution(3990876887654456815)
XLA Ops:
  0.6 53.9 %shard_map.118 = (bf16[3,64,512]{2,1,0:T(8,128)(2,1)}, bf16[3,64,512]{2,1,0:T(8,128)(2,1)}, f32[64,1536]{1,0:T(8,128)}, f32[64,512]{1,0:T(8,128)}, f32[64,1024]{1,0:T(8,128)}, /*index=5*/f32[128,512]{1,0:T(8,128)}) custom-call(bf16[3,64,512]{2,1,0:T(8,128)(2,1)} %refs_0_.1, s32[1,3]{1,0:T(1,128)} %bitcast.1, bf16[3,64,512]{2,1,0:T(8,128)(2,1)} %refs_2_.1, ...), custom_call_target="tpu_custom_call" | custom-call | tf_op jit(solution)/shard_map/pallas_call | solution.py:601
  54.5 2.6 %shard_map.119 = (bf16[3,64,512]{2,1,0:T(8,128)(2,1)}, bf16[3,64,512]{2,1,0:T(8,128)(2,1)}, f32[64,1536]{1,0:T(8,128)}, f32[64,512]{1,0:T(8,128)}, f32[64,1024]{1,0:T(8,128)}, /*index=5*/f32[128,512]{1,0:T(8,128)}) custom-call(bf16[3,64,512]{2,1,0:T(8,128)(2,1)} %get-tuple-element.12.refs_0_, bf16[3,64,512]{2,1,0:T(8,128)(2,1)} %get-tuple-element.13.refs_1_, ...), custom_call_target="tpu_custom_call" | custom-call | tf_op jit(solution)/shard_map/pallas_call | solution.py:611

commit v6 on v5

--- a/solution.py
+++ b/solution.py
@@ -51,8 +51,7 @@
 def head_mean(values, blocks):
     parts = []
     for start in range(0, values.shape[1], QUAD):
-        high, low = split_two(values[:, start : start + QUAD])
-        parts.append(nn(high, blocks) + nn(low, blocks))
+        parts.append(nn(values[:, start : start + QUAD].astype(BF16), blocks))
     return jnp.concatenate(parts, axis=1)
 
 
@@ -413,10 +412,6 @@
     qa[:, 2 * length : 4 * length, :] = query_of(
         jnp.concatenate(normed_far, axis=0)
     )[0].reshape(rows, 2 * length, width)
-    ntr[1] = normed_near.T
-    ntr[2] = jnp.concatenate([piece[:length] for piece in normed_far], axis=0).T
-    ntr[3] = jnp.concatenate([piece[length:] for piece in normed_far], axis=0).T
-    third(0)
     g_across.wait_recv()
     g_onward.start()
     s_across.wait_recv()
@@ -440,9 +435,9 @@
 
     grad_q = head_back(dq_ref[...].reshape(count, width), query_raw, q_inv).astype(BF16)
     lon_send(3, grad_q)
+    third(0)
     for copy in (g_near, s_near, g_onward, s_onward):
         copy.wait_recv()
-    third(1)
 
     for r in range(rows):
         stat = jnp.concatenate([stats[s, r][:, :length] for s in range(SECTORS)], axis=1)
@@ -468,16 +463,17 @@
 
     grad_v = (dv_ref[...].reshape(count, width) * mask_wide).astype(BF16)
     lon_send(4, grad_v)
-    third(2)
-    fourth(0)
     grad_k = head_back(
         dk_ref[...].reshape(count, width) * mask_wide, key_raw, k_inv
     ).astype(BF16)
     lon_send(5, grad_k)
+    third(1)
+    ntr[1] = normed_near.T
+    ntr[2] = jnp.concatenate([piece[:length] for piece in normed_far], axis=0).T
+    ntr[3] = jnp.concatenate([piece[length:] for piece in normed_far], axis=0).T
     lon_sum(3)
-    fourth(1)
-    fourth(2)
-    fifth(0)
+    third(2)
+    fourth(0)
     lon_sum(4)
     grad_normed = (
         nt(grad_q, wqkv[:, :width])
@@ -488,20 +484,21 @@
     store(gt_ref, gt_hbm)
     lon_sum(5)
     fourth(3)
+    fourth(1)
     bo_ref[...] = per_row((middle + mask_wide * nn(active, wdown[...])).astype(BF16))
     store(bo_ref, bo_hbm)
     fourth(4)
+    fifth(0)
+    fourth(2)
+    fourth(5)
+    fifth(3)
     fifth(1)
-    fourth(5)
     finish(0, gdown, 0)
     store(gdown, gdown_hbm)
+    fifth(4)
     fifth(2)
-    fifth(3)
     finish(1, gup, 0)
     store(gup, gup_hbm)
-    fifth(4)
-    finish(2, gout, 0)
-    store(gout, gout_hbm)
     finish(3, gqkv, 0)
     for group in (
         (g_near, g_across, g_onward), (s_near, s_across, s_onward),
@@ -510,6 +507,8 @@
         for copy in group:
             copy.wait_send()
     fifth(5)
+    finish(2, gout, 0)
+    store(gout, gout_hbm)
     finish(4, gqkv, 2 * width)
     finish(5, gqkv, width)
     store(gqkv, gqkv_hbm)

time: 57.2 us -> 56 us (0.979)
  Pallas kernels: 56.4 us -> 55.2 us
    pallas_call x1, Pallas kernels: 53.9 us -> 52.6 us  [local(): pl.pallas_call(functools.partial(kernel, lat_n, scale), out_shape=out_sha...]
where the time goes in v6:
time: 56 us; the launch traced here: 55.8 us
  Pallas kernels  55.2 us (99%)
  between operations  0.64 us (1%)
    pallas_call x1, Pallas kernels, local(): pl.pallas_call(functools.partial(kernel, lat_n, scale), out_shape=out_sha...  52.6 us
    pallas_call x1, Pallas kernels, local(): pl.pallas_call(hand_over, out_shape=out_shape, in_specs=[vmem] * 6, out_s...  2.56 us

profile of v6, /device:TPU:0, one launch (start us, length us, event | category | flops | bytes accessed | tf_op | source)
XLA Modules:
  0.0 55.8 jit_solution(1098028727248010877)
XLA Ops:
  0.6 52.6 %shard_map.118 = (bf16[3,64,512]{2,1,0:T(8,128)(2,1)}, bf16[3,64,512]{2,1,0:T(8,128)(2,1)}, f32[64,1536]{1,0:T(8,128)}, f32[64,512]{1,0:T(8,128)}, f32[64,1024]{1,0:T(8,128)}, /*index=5*/f32[128,512]{1,0:T(8,128)}) custom-call(bf16[3,64,512]{2,1,0:T(8,128)(2,1)} %refs_0_.1, s32[1,3]{1,0:T(1,128)} %bitcast.1, bf16[3,64,512]{2,1,0:T(8,128)(2,1)} %refs_2_.1, ...), custom_call_target="tpu_custom_call" | custom-call | tf_op jit(solution)/shard_map/pallas_call | solution.py:600
  53.3 2.6 %shard_map.119 = (bf16[3,64,512]{2,1,0:T(8,128)(2,1)}, bf16[3,64,512]{2,1,0:T(8,128)(2,1)}, f32[64,1536]{1,0:T(8,128)}, f32[64,512]{1,0:T(8,128)}, f32[64,1024]{1,0:T(8,128)}, /*index=5*/f32[128,512]{1,0:T(8,128)}) custom-call(bf16[3,64,512]{2,1,0:T(8,128)(2,1)} %get-tuple-element.12.refs_0_, bf16[3,64,512]{2,1,0:T(8,128)(2,1)} %get-tuple-element.13.refs_1_, ...), custom_call_target="tpu_custom_call" | custom-call | tf_op jit(solution)/shard_map/pallas_call | solution.py:610
